TPU v7x, 256 devices: a whole 4x4x8 slice. The times are simulated.
256 devices in a mesh: doc: 8 (over z), ctx: 32 (over x, y, core).
Axes of the slice: x: 4, y: 4, z: 8, core: 2. Of those that a mesh axis runs over, the one named last changes fastest.
Arguments:
- queries: bfloat16 [32768, 2048], P(('doc', 'ctx')), parts along dimension 0, may hold values from -8 to 8
- keys: bfloat16 [32768, 2048], P(('doc', 'ctx')), parts along dimension 0, may hold values from -8 to 8
- values: bfloat16 [32768, 2048], P(('doc', 'ctx')), parts along dimension 0, may hold values from -6 to 6
- out_grad: bfloat16 [32768, 2048], P(('doc', 'ctx')), parts along dimension 0, may hold values from -6 to 6
Outputs:
- attended: bfloat16 [32768, 2048], P(('doc', 'ctx')), parts along dimension 0
- query_gradient_array: bfloat16 [32768, 2048], P(('doc', 'ctx')), parts along dimension 0
- key_gradient_array: bfloat16 [32768, 2048], P(('doc', 'ctx')), parts along dimension 0
- value_gradient_array: bfloat16 [32768, 2048], P(('doc', 'ctx')), parts along dimension 0
There are 8 independent parts, one for each index of `doc`. A program takes and returns all parts, laid end to end along the dimension named above; each array names one. Nothing has to cross between parts.
All inputs are finite; a program needn't handle non-finite values.
Results may differ from a plain program's by a relative error of at most 0.025.
The roundings to bfloat16 on the way count: a program that leaves them out, or rounds other values in their place, can miss the bound.
Values may be sent and summed in bfloat16 or wider, within the bound.
A program may use at most 128 MiB of HBM per device.

v0:
```python
import jax
import jax.numpy as jnp
from jax import lax
from jax.sharding import PartitionSpec as P

H = 16
DH = 128
M = 64
ITERS = 6


def softmax_final_axis(scores):
    maxima = jnp.max(scores, axis=-1, keepdims=True)
    expos = jnp.exp(scores - maxima)
    return expos / jnp.sum(expos, axis=-1, keepdims=True)


def batch_product(left, right):
    return jnp.einsum("hij,hjk->hik", left, right, precision=lax.Precision.HIGHEST)


def newton_inverse(amat):
    count = amat.shape[-1]
    colmax = jnp.max(jnp.sum(amat, axis=1), axis=-1)
    rowmax = jnp.max(jnp.sum(amat, axis=2), axis=-1)
    divisor = lax.stop_gradient(colmax * rowmax)
    approx = jnp.swapaxes(amat, 1, 2) / divisor[:, None, None]
    unit_matrix = jnp.eye(count, dtype=amat.dtype)
    for sweep in range(ITERS):
        product = batch_product(amat, approx)
        middle = 7.0 * unit_matrix - product
        middle = 15.0 * unit_matrix - batch_product(product, middle)
        middle = 13.0 * unit_matrix - batch_product(product, middle)
        approx = 0.25 * batch_product(approx, middle)
    return approx


def per_device(queries, keys, values, out_grad):
    running_highest = lax.Precision.HIGHEST
    single_device_result = jnp.float32
    row_count = queries.shape[0]
    group_size = lax.axis_size("ctx")
    own_count = M // group_size
    seg_rows = row_count // own_count
    scale_factor = DH ** (-0.5)
    query_per_head = queries.reshape(row_count, H, DH)
    key_per_head = keys.reshape(row_count, H, DH)
    value_per_head = values.reshape(row_count, H, DH)
    output_gradient_heads = out_grad.reshape(row_count, H, DH)
    query_mean = jnp.mean(
        query_per_head.reshape(own_count, seg_rows, H, DH), axis=1, dtype=single_device_result
    )
    key_mean = jnp.mean(
        key_per_head.reshape(own_count, seg_rows, H, DH), axis=1, dtype=single_device_result
    )
    query_mean = query_mean.astype(jnp.bfloat16).reshape(own_count, H * DH)
    key_mean = key_mean.astype(jnp.bfloat16).reshape(own_count, H * DH)
    query_all, key_all = (
        lax.all_gather(query_mean, "ctx", axis=0, tiled=True),
        lax.all_gather(key_mean, "ctx", axis=0, tiled=True),
    )
    landmark_query_rows = query_all.reshape(M, H, DH)
    landmark_key_rows = key_all.reshape(M, H, DH)
    left_kernel_probs = softmax_final_axis(
        jnp.einsum(
            "ylu,blu->lyb",
            query_per_head,
            landmark_key_rows,
            preferred_element_type=single_device_result,
        )
        * scale_factor
    )
    left_kernel_reduced = left_kernel_probs.astype(jnp.bfloat16)
    a_prob = softmax_final_axis(
        jnp.einsum(
            "ihd,jhd->hij",
            landmark_query_rows,
            landmark_key_rows,
            preferred_element_type=single_device_result,
        )
        * scale_factor
    )
    b_scores = (
        jnp.einsum(
            "spe,bpe->psb",
            landmark_query_rows,
            key_per_head,
            preferred_element_type=single_device_result,
        )
        * scale_factor
    )
    local_max = jnp.max(b_scores, axis=-1)
    value_broad_matrix = value_per_head.astype(single_device_result)
    maxima = lax.pmax(local_max, "ctx")
    weight_tensors = jnp.exp(b_scores - maxima[..., None])
    running_partial_total = jnp.einsum(
        "ioq,qif->iof", weight_tensors, value_broad_matrix, precision=running_highest
    )
    totals, summed_c = lax.psum((jnp.sum(weight_tensors, axis=-1), running_partial_total), "ctx")
    middle_kernel_probs = weight_tensors / totals[..., None]
    right_kernel_matrix = summed_c / totals[..., None]
    pseudo_inverse_matrix, newton_back = jax.vjp(newton_inverse, a_prob)
    context_reduced = batch_product(pseudo_inverse_matrix, right_kernel_matrix).astype(jnp.bfloat16)
    attended = jnp.einsum(
        "pbk,pkj->bpj",
        left_kernel_reduced,
        context_reduced,
        preferred_element_type=single_device_result,
    ).astype(jnp.bfloat16)
    left_kernel_gradient = jnp.einsum(
        "oge,gye->goy",
        output_gradient_heads,
        context_reduced,
        preferred_element_type=single_device_result,
    )
    context_partial = jnp.einsum(
        "spx,pst->sxt",
        left_kernel_reduced,
        output_gradient_heads,
        preferred_element_type=single_device_result,
    )
    context_gradient = lax.psum(context_partial, "ctx")
    pseudo_inverse_gradient = jnp.einsum(
        "uqg,usg->uqs", context_gradient, right_kernel_matrix, precision=running_highest
    )
    right_kernel_gradient = jnp.einsum(
        "gwn,gwe->gne", pseudo_inverse_matrix, context_gradient, precision=running_highest
    )
    (a_grad,) = newton_back(pseudo_inverse_gradient)
    right_kernel_reduced = right_kernel_gradient.astype(jnp.bfloat16)
    middle_kernel_gradient = jnp.einsum(
        "wcv,swv->wcs",
        right_kernel_reduced,
        value_per_head,
        preferred_element_type=single_device_result,
    )
    b_dot = lax.psum(jnp.sum(middle_kernel_probs * middle_kernel_gradient, axis=-1), "ctx")
    middle_kernel_logits = (
        middle_kernel_probs * (middle_kernel_gradient - b_dot[..., None])
    ).astype(jnp.bfloat16)
    value_gradient_array = jnp.einsum(
        "tye,tyc->etc",
        middle_kernel_probs.astype(jnp.bfloat16),
        right_kernel_reduced,
        preferred_element_type=single_device_result,
    ).astype(jnp.bfloat16)
    left_kernel_logits = (
        left_kernel_probs
        * (
            left_kernel_gradient
            - jnp.sum(left_kernel_probs * left_kernel_gradient, axis=-1, keepdims=True)
        )
    ).astype(jnp.bfloat16)
    a_score = a_prob * (a_grad - jnp.sum(a_prob * a_grad, axis=-1, keepdims=True))
    qland_local = (
        jnp.einsum(
            "gab,bgo->ago",
            middle_kernel_logits,
            key_per_head,
            preferred_element_type=single_device_result,
        )
        * scale_factor
    )
    kland_local = (
        jnp.einsum(
            "ksi,ska->ika",
            left_kernel_logits,
            query_per_head,
            preferred_element_type=single_device_result,
        )
        * scale_factor
    )
    qland_common = (
        jnp.einsum(
            "hij,jhd->ihd",
            a_score,
            landmark_key_rows.astype(single_device_result),
            precision=running_highest,
        )
        * scale_factor
    )
    kland_common = (
        jnp.einsum(
            "hij,ihd->jhd",
            a_score,
            landmark_query_rows.astype(single_device_result),
            precision=running_highest,
        )
        * scale_factor
    )
    start = lax.axis_index("ctx") * own_count
    qland_whole, kland_whole = (
        lax.psum(qland_local.astype(jnp.bfloat16), "ctx").astype(jnp.float32),
        lax.psum(kland_local.astype(jnp.bfloat16), "ctx").astype(jnp.float32),
    )
    qland_own = lax.dynamic_slice_in_dim(qland_whole, start, own_count, 0)
    kland_own = lax.dynamic_slice_in_dim(kland_whole, start, own_count, 0)
    qland_own = qland_own + lax.dynamic_slice_in_dim(qland_common, start, own_count, 0)
    kland_own = kland_own + lax.dynamic_slice_in_dim(kland_common, start, own_count, 0)
    query_gradient_array = (
        jnp.einsum(
            "spg,gsu->psu",
            left_kernel_logits,
            landmark_key_rows,
            preferred_element_type=single_device_result,
        )
        * scale_factor
    )
    query_gradient_array = (
        query_gradient_array.reshape(own_count, seg_rows, H, DH) + (qland_own / seg_rows)[:, None]
    )
    key_gradient_array = (
        jnp.einsum(
            "zlk,lzw->kzw",
            middle_kernel_logits,
            landmark_query_rows,
            preferred_element_type=single_device_result,
        )
        * scale_factor
    )
    key_gradient_array = (
        key_gradient_array.reshape(own_count, seg_rows, H, DH) + (kland_own / seg_rows)[:, None]
    )
    width = H * DH
    return (
        attended.reshape(row_count, width),
        query_gradient_array.astype(jnp.bfloat16).reshape(row_count, width),
        key_gradient_array.astype(jnp.bfloat16).reshape(row_count, width),
        value_gradient_array.reshape(row_count, width),
    )


def solution(mesh):
    placed = (
        P(("doc", "ctx"), None),
        P(("doc", "ctx"), None),
        P(("doc", "ctx"), None),
        P(("doc", "ctx"), None),
    )
    return jax.shard_map(
        per_device,
        mesh=mesh,
        in_specs=placed,
        out_specs=(
            P(("doc", "ctx"), None),
            P(("doc", "ctx"), None),
            P(("doc", "ctx"), None),
            P(("doc", "ctx"), None),
        ),
        check_vma=False,
    )
```

profile of v0, /device:TPU:1, one launch (start us, length us, event | category | flops | bytes accessed | tf_op | source)
XLA Modules:
  0.0 665.0 jit_solution(10844618542653295824)
XLA Ops:
  7.2 1.2 convert_bitcast_fusion.1
  8.7 26.6 %all-gather = bf16[32,2,2048]{2,1,0:T(2,128)(2,1)S(1)} all-gather(bf16[1,2,2048]{2,1,0:T(2,128)(2,1)S(1)} %reshape.104), channel_id=1, replica_groups=mesh['doc'=8,'ctx'=32] {'ctx'}, dimensions={0}, use_global_device_ids=true | all-gather | bytes 270336 | tf_op jit(solution)/shard_map/all_gather | solution.py:59
  35.9 24.3 %all-gather.1 = bf16[32,2,2048]{2,1,0:T(2,128)(2,1)S(1)} all-gather(bf16[1,2,2048]{2,1,0:T(2,128)(2,1)S(1)} %reshape.106), channel_id=1, replica_groups=mesh['doc'=8,'ctx'=32] {'ctx'}, dimensions={0}, use_global_device_ids=true | all-gather | bytes 270336 | tf_op jit(solution)/shard_map/all_gather | solution.py:60
  62.9 120.9 %pmax.7 = f32[16,64]{0,1:T(8,128)S(1)} all-reduce(f32[16,64]{0,1:T(8,128)S(1)} %fusion.52), channel_id=1, replica_groups=mesh['doc'=8,'ctx'=32] {'ctx'}, use_global_device_ids=true, to_apply=%region_9.0 | all-reduce | flops 1024 | bytes 8192 | tf_op jit(solution)/shard_map/pmax | solution.py:94
  183.8 1.1 fusion.113
  185.6 1.1 copy.224
  186.8 1.1 fusion.35
  189.3 1.2 fusion.105
  192.8 1.2 convolution_multiply_fusion.8
  194.0 1.0 fusion.110
  197.3 1.0 fusion.109
  200.6 1.0 fusion.108
  204.1 1.0 fusion.107
  208.2 1.0 fusion.106
  209.2 1.4 convolution_subtract_fusion.1
  210.6 124.2 %psum.43 = f32[16,64]{0,1:T(8,128)S(1)} all-reduce(f32[16,64]{0,1:T(8,128)} %get-tuple-element.30), channel_id=1, replica_groups=mesh['doc'=8,'ctx'=32] {'ctx'}, use_global_device_ids=true, to_apply=%region_12.0 | all-reduce | flops 1024 | bytes 8192 | tf_op jit(solution)/shard_map/psum | solution.py:99
  334.9 1.9 convolution_subtract_fusion
  337.6 1.4 convolution_multiply_fusion.3
  339.0 2.2 convolution_convert_fusion.2
  342.5 1.2 fusion.103
  343.7 1.1 convolution_multiply_fusion.2
  345.8 1.0 convolution_negate_fusion.17
  347.9 1.0 convolution_negate_fusion.16
  349.0 1.0 convolution_negate_fusion.15
  350.0 1.0 fusion.12
  353.0 1.2 convolution_negate_fusion.14
  355.3 1.0 convolution_negate_fusion.13
  356.3 1.0 convolution_negate_fusion.12
  357.4 1.0 fusion.10
  360.6 1.0 convolution_negate_fusion.11
  362.7 1.0 convolution_negate_fusion.10
  363.7 1.0 convolution_negate_fusion.9
  364.7 1.0 fusion.8
  366.9 1.4 fusion.124
  368.3 1.0 convolution_negate_fusion.8
  370.3 1.0 convolution_negate_fusion.7
  371.4 1.0 convolution_negate_fusion.6
  372.4 1.0 fusion.6
  375.7 1.0 convolution_negate_fusion.5
  377.7 1.0 convolution_negate_fusion.4
  378.7 1.0 convolution_negate_fusion.3
  379.7 1.0 fusion.4
  381.9 1.8 fusion.128
  384.7 1.8 fusion.127
  386.5 1.8 convolution_negate_fusion.1
  388.4 1.8 fusion.117
  390.1 1.5 convolution_convert_fusion.3
  391.6 123.7 %psum.45 = f32[16,64]{0,1:T(8,128)S(1)} all-reduce(f32[16,64]{0,1:T(8,128)S(1)} %get-tuple-element.35), channel_id=1, replica_groups=mesh['doc'=8,'ctx'=32] {'ctx'}, use_global_device_ids=true, to_apply=%region_18.0 | all-reduce | flops 1024 | bytes 8192 | tf_op jit(solution)/shard_map/psum | solution.py:137
  515.4 1.5 multiply_convert_fusion
  517.8 1.3 convolution_multiply_fusion
  519.2 1.0 convolution_negate_fusion
  525.0 1.0 fusion.2
  526.1 1.2 convolution_add_fusion.1
  528.1 1.3 fusion.84
  529.3 1.4 fusion.85
  535.0 1.3 fusion.63
  536.3 1.0 fusion.64
  538.3 1.1 convolution_convert_fusion
  539.4 1.3 copy.273
  541.8 1.0 copy.276
  542.8 1.0 copy.275
  545.5 108.5 %all-reduce.7.cloned.1.call-done = (bf16[64,16,128]{2,1,0:T(8,128)(2,1)}, bf16[64,16,128]{2,1,0:T(8,128)(2,1)}) async-done(((bf16[64,16,128]{2,1,0:T(8,128)(2,1)}, bf16[64,16,128]{2,1,0:T(8,128)(2,1)}), (bf16[64,16,128]{2,1,0:T(8,128)(2,1)}, bf16[64,16,128]{2,1,0:T(8,128)(2,1)})) %all-reduce.7.cloned.1.call-update) | async-done | bytes 524304 | tf_op jit(solution)/shard_map/psum | solution.py:193
  654.9 1.2 fusion.13
  656.8 1.2 fusion.14
  (249 shorter events, 52.0 us)
Async XLA Ops:
  7.2 177.7 %copy-start = (bf16[128,2048]{1,0:T(8,128)(2,1)S(1)}, bf16[128,2048]{1,0:T(8,128)(2,1)}, u32[]{:S(2)}) copy-start(bf16[128,2048]{1,0:T(8,128)(2,1)} %param.6) | copy-start | bytes 1572868
  7.2 331.8 %all-reduce.5.cloned.1.call-start = ((), (), s32[]{:S(2)}) async-start(), calls=%async_computation | async-start | bytes 2097152 | tf_op jit(solution)/shard_map/psum | solution.py:99
  8.7 26.8 %copy-start.43 = (bf16[128,2048]{1,0:T(8,128)(2,1)S(1)}, bf16[128,2048]{1,0:T(8,128)(2,1)}, u32[]{:S(2)}) copy-start(bf16[128,2048]{1,0:T(8,128)(2,1)} %param.5) | copy-start | bytes 1572868
  35.5 152.7 %copy-start.63 = (bf16[64,16,128]{2,1,0:T(8,128)(2,1)}, bf16[64,16,128]{2,1,0:T(8,128)(2,1)S(1)}, u32[]{:S(2)}) copy-start(bf16[64,16,128]{2,1,0:T(8,128)(2,1)S(1)} %reshape.92) | copy-start | bytes 786436
  35.9 24.5 %copy-start.45 = (bf16[128,2048]{1,0:T(8,128)(2,1)S(1)}, bf16[128,2048]{1,0:T(8,128)(2,1)}, u32[]{:S(2)}) copy-start(bf16[128,2048]{1,0:T(8,128)(2,1)} %param.4) | copy-start | bytes 1572868
  62.0 124.8 %copy-start.65 = (bf16[16,128,64]{1,0,2:T(8,128)(2,1)}, bf16[16,128,64]{1,0,2:T(8,128)(2,1)S(1)}, u32[]{:S(2)}) copy-start(bf16[16,128,64]{1,0,2:T(8,128)(2,1)S(1)} %fusion.104) | copy-start | bytes 786436
  185.6 1.2 copy-start.73
  187.9 466.1 %all-reduce.7.cloned.1.call-start = ((), (), s32[]{:S(2)}) async-start(), calls=%async_computation.1 | async-start | bytes 1048576 | tf_op jit(solution)/shard_map/psum | solution.py:193
  188.8 3.0 copy-start.81
  194.0 2.3 copy-start.47
  197.3 2.3 copy-start.14
  200.6 2.6 copy-start.16
  204.1 3.3 copy-start.19
  208.2 1.0 copy-start.8
  209.2 1.5 copy-start.4
  334.9 2.7 copy-start.9
  341.2 1.1 copy-start.12
  341.2 1.3 copy-start.79
  341.9 1.7 copy-start.51
  342.5 1.2 copy-start.72
  343.7 1.1 copy-start.42
  344.8 1.0 copy-start.10
  345.8 1.0 copy-start.40
  346.9 1.0 copy-start.5
  351.0 1.0 copy-start.39
  352.0 1.0 copy-start.20
  353.0 1.2 copy-start.37
  354.3 1.0 copy-start.3
  358.4 1.2 copy-start.35
  359.6 1.0 copy-start.17
  360.6 1.0 copy-start.33
  365.7 1.2 copy-start.31
  366.9 1.4 copy-start.15
  368.3 1.0 copy-start.29
  373.4 1.2 copy-start.27
  374.6 1.0 copy-start.48
  375.6 1.0 copy-start.25
  380.7 1.2 copy-start.71
  381.9 1.8 copy-start.82
  383.7 1.0 copy-start.23
  388.4 1.8 copy-start.50
  390.1 125.2 %copy-start.13 = (f32[16,64,128]{2,0,1:T(8,128)S(1)}, f32[16,64,128]{2,0,1:T(8,128)}, u32[]{:S(2)}) copy-start(f32[16,64,128]{2,0,1:T(8,128)} %copy-done.11) | copy-start | bytes 1572868
  515.3 1.5 copy-start.44
  517.8 1.3 copy-start.52
  519.2 1.0 copy-start.21
  519.2 1.2 copy-start.54
  519.2 1.4 copy-start.76
  520.5 1.0 copy-start.18
  520.5 1.2 copy-start.56
  521.7 1.0 copy-start.58
  522.8 1.0 copy-start.49
  522.8 1.2 copy-start.60
  524.0 1.0 copy-start.75
  525.0 1.0 copy-start.83
  526.1 1.2 copy-start.80
  529.3 1.4 copy-start.69
  529.3 1.4 copy-start.74
  530.7 1.0 copy-start.7
  532.4 1.0 copy-start.46
  535.0 2.3 copy-start.78
  536.3 3.1 copy-start.61
  540.8 1.0 copy-start.77
  542.8 112.0 %copy-start.62 = (f32[128,2048]{1,0:T(8,128)S(1)}, f32[128,2048]{1,0:T(8,128)}, u32[]{:S(2)}) copy-start(f32[128,2048]{1,0:T(8,128)} %copy.273) | copy-start | bytes 3145732
  656.8 1.2 copy-start.1
  (22 other events, 18.1 us)
Sparse Core Ops, SparseCore 0:
  188.0 117.8 all-reduce.4
  537.5 116.5 all-reduce.6
where the time goes:
time: 673 us; the launch traced here: 665 us
  blocking collectives  420 us (62%)
  waiting for transfers between devices  109 us (16%)
  matrix products  86 us (13%)
  local copies, waits for them, and re-layouts  20.5 us (3%)
  between operations  15.5 us (2%)
  other arithmetic  14.6 us (2%)
    psum x1, blocking collectives, per_device(): lax.psum((jnp.sum(weight_tensors, axis=-1), running_partial_total), 'ctx')  124 us
    psum x1, blocking collectives, per_device(): lax.psum(jnp.sum(middle_kernel_probs * middle_kernel_gradient, axis=-1),...  124 us
    pmax x1, blocking collectives, per_device(): maxima = lax.pmax(local_max, 'ctx')  121 us
    psum x1, waiting for transfers between devices, per_device(): lax.psum(qland_local.astype(jnp.bfloat16), 'ctx').astype(jnp.float32)  109 us
    dot_general x73, matrix products, batch_product(): jnp.einsum('hij,hjk->hik', left, right, precision=lax.Precision.HIGHEST)  72.5 us
    all_gather x1, blocking collectives, per_device(): lax.all_gather(query_mean, 'ctx', axis=0, tiled=True)  26.6 us
    all_gather x1, blocking collectives, per_device(): lax.all_gather(key_mean, 'ctx', axis=0, tiled=True)  24.3 us
    unnamed x174, local copies, waits for them, and re-layouts  15.3 us
  transfers between devices with their start and end apart: 2, of which 1 were waited for; matrix products, arithmetic and copies ran while one was open for 4% of the time, Pallas kernels for 0%

commit v1 on v0

v1 whole, which is shorter than its diff:
```python
import jax
import jax.numpy as jnp
from jax import lax
from jax.experimental import pallas as pl
from jax.experimental.pallas import tpu as pltpu
from jax.sharding import PartitionSpec as P

H = 16
DH = 128
M = 64
ITERS = 6
SCALE = DH ** (-0.5)
MESH = pl.DeviceIdType.MESH
HIGHEST = lax.Precision.HIGHEST
BF = jnp.bfloat16
F32 = jnp.float32
NX, NY, NC = 4, 4, 2
CHIPS = NX * NY
GROUP = CHIPS * NC
ROWS = 128
SEG = 64
WIDTH = H * DH
MSG = 72

OFFSETS = [
    (dx, dy, dc)
    for dx in (2, 1, 3, 0)
    for dy in (2, 1, 3, 0)
    for dc in (0, 1)
    if (dx, dy, dc) != (0, 0, 0)
]


def nn(a, b, precision=None):
    return lax.dot_general(
        a, b, (((1,), (0,)), ((), ())), precision=precision, preferred_element_type=F32
    )


def nt(a, b, precision=None):
    return lax.dot_general(
        a, b, (((1,), (1,)), ((), ())), precision=precision, preferred_element_type=F32
    )


def tn(a, b, precision=None):
    return lax.dot_general(
        a, b, (((0,), (0,)), ((), ())), precision=precision, preferred_element_type=F32
    )


def iota(shape, dim):
    return lax.broadcasted_iota(jnp.int32, shape, dim)


def wait_bytes(ref, sem):
    pltpu.make_async_copy(ref, ref, sem).wait()


def head_cols(h):
    return pl.ds(pl.multiple_of(h * DH, DH), DH)


def kernel(
    q_hbm, k_hbm, v_hbm, g_hbm,
    att_hbm, qg_hbm, kg_hbm, vg_hbm,
    q_v, k_v, v_v, g_v,
    msg32, msg16, rb, lf, ql, kl,
    f_s, w_s, m_s, part, inbox, comb, fin,
    res, stat, cmat_in, cmat_out, ab, sb,
    s32, s16, r4, fs_s, bs_s, bl_s, asc_s,
    att_v, vg_v, qg32, kg32, qg_v, kg_v,
    in_sem, out_sem, e1_s, e1_r, sw_s, sw_r, e2_s, e2_r,
    cm_s, cm_r, e3_s, e3_r, e3t_s, e3t_r, e4_s, e4_r,
):
    me = lax.axis_index("ctx")
    core = lax.rem(me, NC)
    chip = me // NC
    y = lax.rem(chip, NY)
    x = chip // NY

    def peer(offset):
        dx, dy, dc = offset
        return (
            (lax.rem(x + dx, NX) * NY + lax.rem(y + dy, NY)) * NC + lax.rem(core + dc, NC)
        )

    partner = chip * NC + (1 - core)

    def remote(src, dst, send, recv, target):
        return pltpu.make_async_remote_copy(
            src_ref=src, dst_ref=dst, send_sem=send, recv_sem=recv,
            device_id={"ctx": target}, device_id_type=MESH,
        )

    barrier = pltpu.get_barrier_semaphore()
    for offset in OFFSETS:
        pl.semaphore_signal(
            barrier, inc=1, device_id={"ctx": peer(offset)}, device_id_type=MESH
        )
    loads = []
    for slot, (src, dst) in enumerate(
        ((q_hbm, q_v), (k_hbm, k_v), (v_hbm, v_v), (g_hbm, g_v))
    ):
        copy = pltpu.make_async_copy(src, dst, in_sem.at[slot])
        copy.start()
        loads.append(copy)

    pick = jnp.where(iota((8, ROWS), 0) == iota((8, ROWS), 1) // SEG, 1.0, 0.0).astype(BF)
    for which, ref in ((0, q_v), (1, k_v)):
        loads[which].wait()
        sums = nn(pick, ref[...]) * (1.0 / SEG)
        for seg in range(2):
            for h in range(H):
                row = which * 32 + seg * H + h
                msg32[row : row + 1, :] = sums[seg : seg + 1, h * DH : (h + 1) * DH]
    msg16[...] = msg32[...].astype(BF)
    rb[me] = msg16[...]
    pl.semaphore_wait(barrier, GROUP - 1)
    for offset in OFFSETS:
        remote(msg16, rb.at[me], e1_s, e1_r, peer(offset)).start()
    loads[2].wait()
    loads[3].wait()
    wait_bytes(rb.at[0 : GROUP - 1], e1_r)

    for d in range(GROUP):
        for which in range(2):
            lf[which, d * 32 : (d + 1) * 32, :] = rb[d, which * 32 : (which + 1) * 32, :].astype(F32)

    row_at = iota((M, DH), 0)
    lane_at = iota((M, DH), 1)
    diag_low = lane_at == row_at
    diag_high = lane_at == row_at + M

    def landmarks(which, h):
        return lf[which, pl.ds(h, M, stride=H), :].astype(BF)

    def to_col(row):
        return jnp.sum(jnp.where(diag_low, row, 0.0), axis=1, keepdims=True)

    m_s[...] = jnp.zeros_like(m_s)

    def local_group(heads):
        kls, qls, sfs, sbs = [], [], [], []
        for h in heads:
            kl_h = landmarks(1, h)
            ql_h = landmarks(0, h)
            kls.append(kl_h)
            qls.append(ql_h)
            sfs.append(nt(kl_h, q_v[:, head_cols(h)]) * SCALE)
            sbs.append(nt(ql_h, k_v[:, head_cols(h)]) * SCALE)
        fps, gps = [], []
        for h, sf in zip(heads, sfs):
            e = jnp.exp(sf - jnp.max(sf, axis=0, keepdims=True))
            fp = e / jnp.sum(e, axis=0, keepdims=True)
            fps.append(fp)
            gps.append(nn(fp.astype(BF), g_v[:, head_cols(h)]))
        ws, cps, rows, ms = [], [], [], []
        for h, s in zip(heads, sbs):
            m = jnp.max(s, axis=1, keepdims=True)
            w = jnp.exp(s - m)
            t = jnp.sum(w, axis=1, keepdims=True)
            hi = w.astype(BF)
            lo = (w - hi.astype(F32)).astype(BF)
            vals = v_v[:, head_cols(h)]
            cps.append(nn(hi, vals) + nn(lo, vals))
            rows.append(
                jnp.sum(
                    jnp.where(diag_low, m, 0.0) + jnp.where(diag_high, t, 0.0),
                    axis=0, keepdims=True,
                )
            )
            ws.append(w)
            ms.append(m)
        known = m_s[...]
        for h, m in zip(heads, ms):
            known = jnp.where(lane_at == h, m, known)
        m_s[...] = known
        for j, h in enumerate(heads):
            kl[h] = kls[j]
            ql[h] = qls[j]
            f_s[h] = fps[j]
            w_s[h] = ws[j]
            part[0, h, 0:M, :] = cps[j]
            part[0, h, M:MSG, :] = jnp.broadcast_to(rows[j], (MSG - M, DH))
            part[1, h, 0:M, :] = gps[j]
            part[1, h, M:MSG, :] = jnp.zeros((MSG - M, DH), F32)

    def combine(heads):
        out = []
        for h in heads:
            row0 = part[core, h, M : M + 1, :]
            row1 = inbox[h, M : M + 1, :]
            top = jnp.maximum(row0, row1)
            f0 = jnp.exp(row0 - top)
            f1 = jnp.exp(row1 - top)
            t = pltpu.roll(f0, M, 1) * row0 + pltpu.roll(f1, M, 1) * row1
            row = jnp.where(iota((1, DH), 1) < M, top, t)
            total = part[core, h, 0:M, :] * to_col(f0) + inbox[h, 0:M, :] * to_col(f1)
            out.append((total, row))
        for h, (total, row) in zip(heads, out):
            comb[h, 0:M, :] = total
            comb[h, M:MSG, :] = jnp.broadcast_to(row, (MSG - M, DH))

    def group_of(i):
        return lax.rem(x + 1 + i, NX)

    def heads_of(i):
        return [group_of(i) * NY + lax.rem(y + 1 + j, NY) for j in range(NY)]

    swaps = []

    def finish(i):
        swaps[i].wait_recv()
        heads = heads_of(i)
        combine(heads)
        for j, h in enumerate(heads):
            if i == NX - 1 and j == NY - 1:
                fin[chip] = comb[h]
            else:
                remote(comb.at[h], fin.at[chip], e2_s, e2_r, h * NC + core).start()

    for i in range(NX):
        local_group(heads_of(i))
        block = pl.ds(group_of(i) * NY, NY)
        swap = remote(
            part.at[1 - core, block], inbox.at[block], sw_s.at[i], sw_r.at[i], partner
        )
        swap.start()
        swaps.append(swap)
        if i > 0:
            finish(i - 1)
    finish(NX - 1)

    ql_own = ql[chip]
    kl_own = kl[chip]
    scores = nt(ql_own, kl_own) * SCALE
    e = jnp.exp(scores - jnp.max(scores, axis=1, keepdims=True))
    a = e / jnp.sum(e, axis=1, keepdims=True)
    divisor = jnp.max(jnp.sum(a, axis=0, keepdims=True), axis=1, keepdims=True) * jnp.max(
        jnp.sum(a, axis=1, keepdims=True), axis=0, keepdims=True
    )
    a_t = a.T
    z = a_t / divisor
    unit = jnp.where(iota((M, M), 0) == iota((M, M), 1), 1.0, 0.0)
    sweeps = []
    for _ in range(ITERS):
        p = nn(a, z, HIGHEST)
        q1 = 7.0 * unit - p
        q2 = 15.0 * unit - nn(p, q1, HIGHEST)
        q3 = 13.0 * unit - nn(p, q2, HIGHEST)
        sweeps.append((z.T, p.T, q1, q2, q3))
        z = 0.25 * nn(z, q3, HIGHEST)
    left = jnp.where(core == 0, z, z.T)

    wait_bytes(fin.at[0 : CHIPS - 1], e2_r)
    rows = jnp.concatenate([fin[s, M : M + 1, :] for s in range(CHIPS)], axis=0)
    top = jnp.max(rows, axis=0, keepdims=True)
    factor = jnp.exp(rows - top)
    total = jnp.sum(factor * pltpu.roll(rows, M, 1), axis=0, keepdims=True)
    low = iota((1, DH), 1) < M
    inverse = jnp.where(low, 1.0 / jnp.where(low & (core == 0), total, 1.0), 0.0)
    eye_low = jnp.where(diag_low, 1.0, 0.0)
    weight = nt(eye_low, factor * inverse, HIGHEST)
    summed = fin[0, 0:M, :] * weight[:, 0:1]
    for s in range(1, CHIPS):
        summed = summed + fin[s, 0:M, :] * weight[:, s : s + 1]
    made = nn(left, summed, HIGHEST).astype(BF)
    res[...] = made
    ab[me] = made
    for offset in OFFSETS:
        remote(res, ab.at[me], e3_s, e3_r, peer(offset)).start()

    def send_stat():
        sb[me] = stat[...]
        for offset in OFFSETS:
            remote(stat, sb.at[me], e3t_s, e3t_r, peer(offset)).start()

    @pl.when(core == 0)
    def _():
        cmat_out[...] = summed
        remote(cmat_out, cmat_in, cm_s, cm_r, partner).start()
        stat[...] = jnp.where(iota((8, DH), 0) == 0, top, inverse)
        send_stat()
        wait_bytes(cmat_out, cm_s)

    @pl.when(core == 1)
    def _():
        wait_bytes(cmat_in, cm_r)
        c = cmat_in[...]
        dots = jnp.sum(made.astype(F32) * c, axis=1, keepdims=True)
        stat[...] = jnp.broadcast_to(
            jnp.sum(jnp.where(diag_low, dots, 0.0), axis=0, keepdims=True), (8, DH)
        )
        send_stat()
        grad = nt(summed, c, HIGHEST)
        a_grad = jnp.zeros((M, M), F32)
        for z_t, p_t, r1, r2, r3 in sweeps[::-1]:
            d3 = 0.25 * nn(z_t, grad, HIGHEST)
            dz = 0.25 * nt(grad, r3, HIGHEST)
            d2 = -nn(p_t, d3, HIGHEST)
            dp = -nt(d3, r2, HIGHEST) - nt(d2, r1, HIGHEST) + nn(p_t, d2, HIGHEST)
            a_grad = a_grad + nn(dp, z_t, HIGHEST)
            grad = dz + nn(a_t, dp, HIGHEST)
        a_grad = a_grad + grad.T / divisor
        a_score = a * (a_grad - jnp.sum(a * a_grad, axis=1, keepdims=True))
        asc_s[0] = nn(a_score, kl_own.astype(F32), HIGHEST) * SCALE
        asc_s[1] = nn(a_score.T, ql_own.astype(F32), HIGHEST) * SCALE

    wait_bytes(ab.at[0 : GROUP - 1], e3_r)
    wait_bytes(sb.at[0 : GROUP - 1], e3t_r)

    gathered = jnp.concatenate(
        [sb[NC * h, 0:1, :] for h in range(H)]
        + [sb[NC * h, 1:2, :] for h in range(H)]
        + [sb[NC * h + 1, 0:1, :] for h in range(H)],
        axis=0,
    )
    cols = nt(eye_low, gathered, HIGHEST)
    alphas = jnp.exp(m_s[:, 0:H] - cols[:, 0:H]) * cols[:, H : 2 * H]

    for base in range(0, H, 4):
        heads = range(base, base + 4)
        fgs = [nt(ab[NC * h], g_v[:, h * DH : (h + 1) * DH]) for h in heads]
        bgs = [nt(ab[NC * h + 1], v_v[:, h * DH : (h + 1) * DH]) for h in heads]
        outs = []
        for h, fg, bg in zip(heads, fgs, bgs):
            fp = f_s[h]
            fs = (fp * (fg - jnp.sum(fp * fg, axis=0, keepdims=True))).astype(BF)
            bp = w_s[h] * alphas[:, h : h + 1]
            bs = (bp * (bg - cols[:, 2 * H + h : 2 * H + h + 1])).astype(BF)
            kp = nn(fs, q_v[:, h * DH : (h + 1) * DH]) * SCALE
            qp = nn(bs, k_v[:, h * DH : (h + 1) * DH]) * SCALE
            outs.append((fs, bs, bp.astype(BF), qp, kp))
        for h, (fs, bs, bl, qp, kp) in zip(heads, outs):
            fs_s[h] = fs
            bs_s[h] = bs
            bl_s[h] = bl
            s32[0, pl.ds(h, M, stride=H), :] = qp
            s32[1, pl.ds(h, M, stride=H), :] = kp

    @pl.when(core == 1)
    def _():
        for which in range(2):
            at = pl.ds(chip, M, stride=H)
            s32[which, at, :] = s32[which, at, :] + asc_s[which]

    for d in range(GROUP):
        for which in range(2):
            s16[d, which * 32 : (which + 1) * 32, :] = s32[which, d * 32 : (d + 1) * 32, :].astype(BF)
    r4[me] = s16[me]
    for offset in OFFSETS:
        remote(s16.at[peer(offset)], r4.at[me], e4_s, e4_r, peer(offset)).start()

    for h in range(H):
        at = slice(h * DH, (h + 1) * DH)
        att_v[:, at] = tn(f_s[h].astype(BF), ab[NC * h]).astype(BF)
        vg_v[:, at] = tn(bl_s[h], ab[NC * h + 1]).astype(BF)
    out_a = pltpu.make_async_copy(att_v, att_hbm, out_sem.at[0])
    out_v = pltpu.make_async_copy(vg_v, vg_hbm, out_sem.at[3])
    out_a.start()
    out_v.start()
    for h in range(H):
        at = slice(h * DH, (h + 1) * DH)
        qg32[:, at] = tn(fs_s[h], kl[h]) * SCALE
        kg32[:, at] = tn(bs_s[h], ql[h]) * SCALE

    wait_bytes(r4.at[0 : GROUP - 1], e4_r)
    land = r4[0].astype(F32)
    for d in range(1, GROUP):
        land = land + r4[d].astype(F32)
    land = land * (1.0 / SEG)
    for h in range(H):
        at = slice(h * DH, (h + 1) * DH)
        for seg in range(2):
            here = slice(seg * SEG, (seg + 1) * SEG)
            row = seg * H + h
            qg_v[here, at] = (qg32[here, at] + land[row : row + 1, :]).astype(BF)
            kg_v[here, at] = (kg32[here, at] + land[32 + row : 32 + row + 1, :]).astype(BF)
    out_q = pltpu.make_async_copy(qg_v, qg_hbm, out_sem.at[1])
    out_k = pltpu.make_async_copy(kg_v, kg_hbm, out_sem.at[2])
    out_q.start()
    out_k.start()

    wait_bytes(rb.at[0 : GROUP - 1], e1_s)
    for swap in swaps:
        swap.wait_send()
    wait_bytes(fin.at[0 : CHIPS - 1], e2_s)
    wait_bytes(ab.at[0 : GROUP - 1], e3_s)
    wait_bytes(sb.at[0 : GROUP - 1], e3t_s)
    wait_bytes(r4.at[0 : GROUP - 1], e4_s)
    for copy in (out_a, out_v, out_q, out_k):
        copy.wait()


def per_device(queries, keys, values, out_grad):
    shape = (ROWS, WIDTH)
    dma = pltpu.SemaphoreType.DMA
    rows = pltpu.VMEM(shape, BF)
    scratch = (
        [rows] * 4
        + [pltpu.VMEM((64, DH), F32), pltpu.VMEM((64, DH), BF)]
        + [pltpu.VMEM((GROUP, 64, DH), BF), pltpu.VMEM((2, M * H, DH), F32)]
        + [pltpu.VMEM((H, M, DH), BF)] * 2
        + [pltpu.VMEM((H, M, ROWS), F32)] * 2
        + [pltpu.VMEM((M, DH), F32)]
        + [pltpu.VMEM((2, H, MSG, DH), F32)]
        + [pltpu.VMEM((H, MSG, DH), F32)] * 3
        + [pltpu.VMEM((M, DH), BF), pltpu.VMEM((8, DH), F32)]
        + [pltpu.VMEM((M, DH), F32)] * 2
        + [pltpu.VMEM((GROUP, M, DH), BF), pltpu.VMEM((GROUP, 8, DH), F32)]
        + [pltpu.VMEM((2, M * H, DH), F32)]
        + [pltpu.VMEM((GROUP, 64, DH), BF)] * 2
        + [pltpu.VMEM((H, M, ROWS), BF)] * 3
        + [pltpu.VMEM((2, M, DH), F32)]
        + [rows] * 2
        + [pltpu.VMEM(shape, F32)] * 2
        + [rows] * 2
        + [dma((4,)), dma((4,)), dma, dma, dma((NX,)), dma((NX,))]
        + [dma] * 10
    )
    return pl.pallas_call(
        kernel,
        out_shape=[jax.ShapeDtypeStruct(shape, BF)] * 4,
        in_specs=[pl.BlockSpec(memory_space=pl.ANY)] * 4,
        out_specs=[pl.BlockSpec(memory_space=pl.ANY)] * 4,
        scratch_shapes=scratch,
        compiler_params=pltpu.CompilerParams(
            collective_id=0, has_side_effects=True, vmem_limit_bytes=56 << 20
        ),
    )(queries, keys, values, out_grad)


def solution(mesh):
    placed = P(("doc", "ctx"), None)
    return jax.shard_map(
        per_device,
        mesh=mesh,
        in_specs=(placed,) * 4,
        out_specs=(placed,) * 4,
        check_vma=False,
    )
```

time: 673 us -> 55.7 us (0.08); the launches traced: 665 us -> 55.5 us
  blocking collectives: 420 us -> 0 us
  waiting for transfers between devices: 109 us -> 0 us
  matrix products: 86 us -> 0 us
  Pallas kernels: 0 us -> 49.6 us
  local copies, waits for them, and re-layouts: 20.5 us -> 5.19 us
  between operations: 15.5 us -> 0.65 us
  other arithmetic: 14.6 us -> 0 us
    psum x2 -> x0, blocking collectives: 248 us -> none  [the longest x1 124 us: per_device(): lax.psum((jnp.sum(weight_tensors, axis=-1), running_partial_total), 'ctx')]
    pmax x1 -> x0, blocking collectives: 121 us -> none  [per_device(): maxima = lax.pmax(local_max, 'ctx')]
    psum x2 -> x0, waiting for transfers between devices: 109 us -> none  [the longest x1 109 us: per_device(): lax.psum(qland_local.astype(jnp.bfloat16), 'ctx').astype(jnp.float32)]
    dot_general x90 -> x0, matrix products: 86 us -> none  [the longest x73 72.5 us: batch_product(): jnp.einsum('hij,hjk->hik', left, right, precision=lax.Precision.HIGHEST)]
    all_gather x2 -> x0, blocking collectives: 50.8 us -> none  [the longest x1 26.6 us: per_device(): lax.all_gather(query_mean, 'ctx', axis=0, tiled=True)]
    pallas_call x0 -> x1, Pallas kernels: none -> 49.6 us  [per_device(): pl.pallas_call(kernel, out_shape=[jax.ShapeDtypeStruct(shape, BF)] * 4, i...]
    unnamed x174 -> x10, local copies, waits for them, and re-layouts: 15.3 us -> 5.19 us
    convert_element_type x10 -> x0, other arithmetic: 8.33 us -> none  [the longest x1 1.52 us: per_device(): middle_kernel_logits = (middle_kernel_probs * (middle_kernel_gradient - b...]
  transfers between devices with their start and end apart: 2 -> 0, of which waited for: 1 -> 0; matrix products, arithmetic and copies ran while one was open for 4% -> 0% of each run, Pallas kernels for 0% -> 0%
where the time goes in v1:
time: 55.7 us; the launch traced here: 55.5 us
  Pallas kernels  49.6 us (89%)
  local copies, waits for them, and re-layouts  5.19 us (9%)
  between operations  0.65 us (1%)
    pallas_call x1, Pallas kernels, per_device(): pl.pallas_call(kernel, out_shape=[jax.ShapeDtypeStruct(shape, BF)] * 4, i...  49.6 us
    unnamed x10, local copies, waits for them, and re-layouts  5.19 us

profile of v1, /device:TPU:1, one launch (start us, length us, event | category | flops | bytes accessed | tf_op | source)
XLA Modules:
  0.0 55.5 jit_solution(10728741642436190377)
XLA Ops:
  0.6 49.6 %shard_map.75 = (bf16[128,2048]{1,0:T(8,128)(2,1)}, bf16[128,2048]{1,0:T(8,128)(2,1)}, bf16[128,2048]{1,0:T(8,128)(2,1)}, bf16[128,2048]{1,0:T(8,128)(2,1)}) custom-call(bf16[128,2048]{1,0:T(8,128)(2,1)} %q_hbm.1, bf16[128,2048]{1,0:T(8,128)(2,1)} %k_hbm.1, bf16[128,2048]{1,0:T(8,128)(2,1)} %v_hbm.1, bf16[128,2048]{1,0:T(8,128)(2,1)} %g_hbm.1), custom_call_target="tpu_custom_call" | custom-call | tf_op jit(solution)/shard_map/pallas_call | solution.py:422
  50.3 0.0 copy-start.2
  50.3 1.9 %copy.12 = bf16[128,2048]{1,0:T(8,128)(2,1)} copy(bf16[128,2048]{1,0:T(8,128)(2,1)} %get-tuple-element.8) | data formatting | bytes 1048576
  52.2 0.0 copy-done.2
  52.2 0.0 copy-start.1
  52.2 0.8 %copy.13 = bf16[128,2048]{1,0:T(8,128)(2,1)} copy(bf16[128,2048]{1,0:T(8,128)(2,1)S(1)} %copy-done.2) | data formatting | bytes 1048576
  53.0 0.4 copy-done.1
  53.5 0.0 copy-start
  53.5 0.8 %copy.14 = bf16[128,2048]{1,0:T(8,128)(2,1)} copy(bf16[128,2048]{1,0:T(8,128)(2,1)S(1)} %copy-done.1) | data formatting | bytes 1048576
  54.3 0.4 copy-done
  54.7 0.8 %copy.15 = bf16[128,2048]{1,0:T(8,128)(2,1)} copy(bf16[128,2048]{1,0:T(8,128)(2,1)S(1)} %copy-done) | data formatting | bytes 1048576
Async XLA Ops:
  50.3 2.0 %copy-start.2 = (bf16[128,2048]{1,0:T(8,128)(2,1)S(1)}, bf16[128,2048]{1,0:T(8,128)(2,1)}, u32[]{:S(2)}) copy-start(bf16[128,2048]{1,0:T(8,128)(2,1)} %get-tuple-element.9) | copy-start | bytes 1572868
  52.2 1.2 %copy-start.1 = (bf16[128,2048]{1,0:T(8,128)(2,1)S(1)}, bf16[128,2048]{1,0:T(8,128)(2,1)}, u32[]{:S(2)}) copy-start(bf16[128,2048]{1,0:T(8,128)(2,1)} %get-tuple-element.10) | copy-start | bytes 1572868
  53.5 1.2 %copy-start = (bf16[128,2048]{1,0:T(8,128)(2,1)S(1)}, bf16[128,2048]{1,0:T(8,128)(2,1)}, u32[]{:S(2)}) copy-start(bf16[128,2048]{1,0:T(8,128)(2,1)} %get-tuple-element.11) | copy-start | bytes 1572868

commit v2 on v1

v2 whole, which is shorter than its diff:
```python
import jax
import jax.numpy as jnp
from jax import lax
from jax.experimental import pallas as pl
from jax.experimental.pallas import tpu as pltpu
from jax.sharding import PartitionSpec as P

H = 16
DH = 128
M = 64
ITERS = 6
SCALE = DH ** (-0.5)
MESH = pl.DeviceIdType.MESH
HIGHEST = lax.Precision.HIGHEST
BF = jnp.bfloat16
F32 = jnp.float32
NX, NY, NC = 4, 4, 2
CHIPS = NX * NY
GROUP = CHIPS * NC
ROWS = 128
SEG = 64
WIDTH = H * DH

OFFSETS = [
    (dx, dy, dc)
    for dx in (2, 1, 3, 0)
    for dy in (2, 1, 3, 0)
    for dc in (0, 1)
    if (dx, dy, dc) != (0, 0, 0)
]


STEPS = [(dx, dy) for dx, dy, dc in OFFSETS if dc == 0]


def nn(a, b, precision=None):
    return lax.dot_general(
        a, b, (((1,), (0,)), ((), ())), precision=precision, preferred_element_type=F32
    )


def nt(a, b, precision=None):
    return lax.dot_general(
        a, b, (((1,), (1,)), ((), ())), precision=precision, preferred_element_type=F32
    )


def tn(a, b, precision=None):
    return lax.dot_general(
        a, b, (((0,), (0,)), ((), ())), precision=precision, preferred_element_type=F32
    )


def iota(shape, dim):
    return lax.broadcasted_iota(jnp.int32, shape, dim)


def wait_bytes(ref, sem):
    pltpu.make_async_copy(ref, ref, sem).wait()


def head_cols(h):
    return pl.ds(pl.multiple_of(h * DH, DH), DH)


def kernel(
    q_hbm, k_hbm, v_hbm, g_hbm,
    att_v, vg_v, qg32, kg32, land,
    q_v, k_v, v_v, g_v,
    msg32, msg16, rb, lf, ql, kl,
    f_s, w_s, part, inbox, comb, fin, mt_s, mt_in, mt_c, mt_f, sum_s,
    lefts, steps, sides,
    res, stat, cmat_in, cmat_out, ab, sb,
    gpart, ginb, s32, s16, r4, fs_s, bs_s, bl_s, asc_s,
    in_sem, e1_s, e1_r, sw_s, sw_r, mt_ss, mt_sr, e2_s, e2_r, e2t_s, e2t_r,
    cm_s, cm_r, e3_s, e3_r, e3t_s, e3t_r, gs_s, gs_r, e4_s, e4_r,
):
    me = lax.axis_index("ctx")
    core = lax.rem(me, NC)
    chip = me // NC
    y = lax.rem(chip, NY)
    x = chip // NY

    def peer(offset):
        dx, dy, dc = offset
        return (
            (lax.rem(x + dx, NX) * NY + lax.rem(y + dy, NY)) * NC + lax.rem(core + dc, NC)
        )

    partner = chip * NC + (1 - core)

    def remote(src, dst, send, recv, target):
        return pltpu.make_async_remote_copy(
            src_ref=src, dst_ref=dst, send_sem=send, recv_sem=recv,
            device_id={"ctx": target}, device_id_type=MESH,
        )

    def spread(block, slots, send, recv):
        for dx, dy in STEPS:
            remote(
                block, slots.at[core, chip], send.at[NX], recv.at[dx], peer((dx, dy, 0))
            ).start()

    def relay_row(slots, send, recv, dx):
        row = lax.rem(x + NX - dx, NX) * NY
        wait_bytes(slots.at[core, pl.ds(0, NY - 1 if dx == 0 else NY)], recv.at[dx])
        block = slots.at[core, pl.ds(row, NY)]
        copy = remote(block, block, send.at[dx], recv.at[NX + dx], partner)
        copy.start()
        return copy

    def relay(slots, send, recv):
        return [relay_row(slots, send, recv, dx) for dx in (0, 1, 3, 2)]

    def settle(slots, copies, send):
        wait_bytes(slots.at[core, pl.ds(0, CHIPS - 1)], send.at[NX])
        for copy in copies:
            copy.wait_send()

    barrier = pltpu.get_barrier_semaphore()
    for offset in OFFSETS:
        pl.semaphore_signal(
            barrier, inc=1, device_id={"ctx": peer(offset)}, device_id_type=MESH
        )
    loads = []
    for slot, (src, dst) in enumerate(
        ((q_hbm, q_v), (k_hbm, k_v), (v_hbm, v_v), (g_hbm, g_v))
    ):
        copy = pltpu.make_async_copy(src, dst, in_sem.at[slot])
        copy.start()
        loads.append(copy)

    pick = jnp.where(iota((8, ROWS), 0) == iota((8, ROWS), 1) // SEG, 1.0, 0.0).astype(BF)
    for which, ref in ((0, q_v), (1, k_v)):
        loads[which].wait()
        sums = nn(pick, ref[...]) * (1.0 / SEG)
        for seg in range(2):
            for h in range(H):
                row = which * 32 + seg * H + h
                msg32[row : row + 1, :] = sums[seg : seg + 1, h * DH : (h + 1) * DH]
    msg16[...] = msg32[...].astype(BF)
    rb[core, chip] = msg16[...]
    pl.semaphore_wait(barrier, GROUP - 1)
    spread(msg16, rb, e1_s, e1_r)
    loads[2].wait()
    loads[3].wait()
    relays = relay(rb, e1_s, e1_r)
    for copy in relays:
        copy.wait_recv()

    for c in range(NC):
        for d in range(CHIPS):
            for which in range(2):
                at = (d * NC + c) * 32
                lf[which, at : at + 32, :] = rb[c, d, which * 32 : (which + 1) * 32, :].astype(F32)

    row_at = iota((M, DH), 0)
    lane_at = iota((M, DH), 1)
    diag_low = lane_at == row_at
    diag_high = lane_at == row_at + M

    def landmarks(which, h):
        return lf[which, pl.ds(h, M, stride=H), :].astype(BF)

    def to_col(row):
        return jnp.sum(jnp.where(diag_low, row, 0.0), axis=1, keepdims=True)

    low = iota((1, DH), 1) < M
    eye_low = jnp.where(diag_low, 1.0, 0.0)

    def local_group(heads):
        kls, qls, sfs, sbs = [], [], [], []
        for h in heads:
            kl_h = landmarks(1, h)
            ql_h = landmarks(0, h)
            kls.append(kl_h)
            qls.append(ql_h)
            sfs.append(nt(kl_h, q_v[:, head_cols(h)]) * SCALE)
            sbs.append(nt(ql_h, k_v[:, head_cols(h)]) * SCALE)
        fps, gps = [], []
        for h, sf in zip(heads, sfs):
            e = jnp.exp(sf - jnp.max(sf, axis=0, keepdims=True))
            fp = e / jnp.sum(e, axis=0, keepdims=True)
            fps.append(fp)
            gps.append(nn(fp.astype(BF), g_v[:, head_cols(h)]))
        ws, cps, rows = [], [], []
        for h, s in zip(heads, sbs):
            m = jnp.max(s, axis=1, keepdims=True)
            w = jnp.exp(s - m)
            t = jnp.sum(w, axis=1, keepdims=True)
            hi = w.astype(BF)
            lo = (w - hi.astype(F32)).astype(BF)
            vals = v_v[:, head_cols(h)]
            cps.append(nn(hi, vals) + nn(lo, vals))
            rows.append(
                jnp.sum(
                    jnp.where(diag_low, m, 0.0) + jnp.where(diag_high, t, 0.0),
                    axis=0, keepdims=True,
                )
            )
            ws.append(w)
        for j, h in enumerate(heads):
            kl[h] = kls[j]
            ql[h] = qls[j]
            f_s[h] = fps[j]
            w_s[h] = ws[j]
            part[0, h] = cps[j]
            part[1, h] = gps[j]
            mt_s[h] = rows[j]

    def combine(heads):
        @pl.when(core == 0)
        def _():
            out = []
            for h in heads:
                row0 = mt_s[h]
                row1 = mt_in[h]
                top = jnp.maximum(row0, row1)
                f0 = jnp.exp(row0 - top)
                f1 = jnp.exp(row1 - top)
                t = pltpu.roll(f0, M, 1) * row0 + pltpu.roll(f1, M, 1) * row1
                both = part[0, h] * to_col(f0) + inbox[h] * to_col(f1)
                out.append((both, jnp.where(low, top, t)))
            for h, (both, row) in zip(heads, out):
                comb[h] = both
                mt_c[h] = row

        @pl.when(core == 1)
        def _():
            sums = [part[1, h] + inbox[h] for h in heads]
            for h, both in zip(heads, sums):
                comb[h] = both

    def group_of(i):
        return lax.rem(x + 1 + i, NX)

    def heads_of(i):
        return [group_of(i) * NY + lax.rem(y + 1 + j, NY) for j in range(NY)]

    swaps = []

    def finish(i):
        swaps[i].wait_recv()

        @pl.when(core == 0)
        def _():
            here = pl.ds(group_of(i) * NY, NY)
            wait_bytes(mt_in.at[here], mt_sr.at[i])

        heads = heads_of(i)
        combine(heads)
        for j, h in enumerate(heads):
            if i == NX - 1 and j == NY - 1:
                fin[chip] = comb[h]
            else:
                remote(comb.at[h], fin.at[chip], e2_s, e2_r, h * NC + core).start()

        @pl.when(core == 0)
        def _():
            for j, h in enumerate(heads):
                if i == NX - 1 and j == NY - 1:
                    mt_f[chip] = mt_c[h]
                else:
                    remote(mt_c.at[h], mt_f.at[chip], e2t_s, e2t_r, h * NC).start()

    for i in range(NX):
        local_group(heads_of(i))
        block = pl.ds(group_of(i) * NY, NY)

        @pl.when(core == 1)
        def _():
            remote(mt_s.at[block], mt_in.at[block], mt_ss.at[i], mt_sr.at[i], partner).start()

        swap = remote(
            part.at[1 - core, block], inbox.at[block], sw_s.at[i], sw_r.at[i], partner
        )
        swap.start()
        swaps.append(swap)
    for i in range(NX):
        finish(i)

    ql_own = ql[chip]
    kl_own = kl[chip]
    scores = nt(ql_own, kl_own) * SCALE
    e = jnp.exp(scores - jnp.max(scores, axis=1, keepdims=True))
    a = e / jnp.sum(e, axis=1, keepdims=True)
    divisor = jnp.max(jnp.sum(a, axis=0, keepdims=True), axis=1, keepdims=True) * jnp.max(
        jnp.sum(a, axis=1, keepdims=True), axis=0, keepdims=True
    )
    a_t = a.T
    z = a_t / divisor
    unit = jnp.where(iota((M, M), 0) == iota((M, M), 1), 1.0, 0.0)
    sweeps = []
    for _ in range(ITERS):
        p = nn(a, z, HIGHEST)
        q1 = 7.0 * unit - p
        q2 = 15.0 * unit - nn(p, q1, HIGHEST)
        q3 = 13.0 * unit - nn(p, q2, HIGHEST)
        sweeps.append((z, p, q1, q2, q3))
        z = 0.25 * nn(z, q3, HIGHEST)
    left = jnp.where(core == 0, z, z.T)

    @pl.when(core == 1)
    def _():
        for k, (before, p, q1, q2, q3) in enumerate(sweeps):
            l0 = before.T
            l1 = nn(p, l0, HIGHEST)
            l2 = nn(p, l1, HIGHEST)
            s0, s1, s2 = [nn(a_t, l, HIGHEST) for l in (l0, l1, l2)]
            lefts[k] = jnp.concatenate([s0, s1, s2, l0, l1, l2], axis=0)
            steps[k] = 0.25 * jnp.concatenate([q3, -q2, q1, -unit], axis=0)
            sides[k] = 0.25 * jnp.concatenate(
                [7.0 * l1 - 15.0 * l0 - l2, 7.0 * l0 - l1, -l0], axis=0
            )

    wait_bytes(fin.at[0 : CHIPS - 1], e2_r)

    @pl.when(core == 0)
    def _():
        wait_bytes(mt_f.at[0 : CHIPS - 1], e2t_r)
        rows = jnp.concatenate([mt_f[s] for s in range(CHIPS)], axis=0)
        top = jnp.max(rows, axis=0, keepdims=True)
        factor = jnp.exp(rows - top)
        total = jnp.sum(factor * pltpu.roll(rows, M, 1), axis=0, keepdims=True)
        inverse = jnp.where(low, 1.0 / jnp.where(low, total, 1.0), 0.0)
        weight = nt(eye_low, factor * inverse, HIGHEST)
        summed = fin[0] * weight[:, 0:1]
        for s in range(1, CHIPS):
            summed = summed + fin[s] * weight[:, s : s + 1]
        sum_s[...] = summed
        stat[...] = jnp.where(low, top, pltpu.roll(inverse, M, 1))

    @pl.when(core == 1)
    def _():
        summed = fin[0]
        for s in range(1, CHIPS):
            summed = summed + fin[s]
        sum_s[...] = summed

    summed = sum_s[...]
    made = nn(left, summed, HIGHEST).astype(BF)
    res[...] = made
    ab[core, chip] = made
    spread(res, ab, e3_s, e3_r)

    def send_stat():
        sb[me] = stat[...]
        for offset in OFFSETS:
            remote(stat, sb.at[me], e3t_s, e3t_r.at[offset[0]], peer(offset)).start()

    @pl.when(core == 0)
    def _():
        cmat_out[...] = summed
        remote(cmat_out, cmat_in, cm_s, cm_r, partner).start()
        send_stat()
        wait_bytes(cmat_out, cm_s)

    @pl.when(core == 1)
    def _():
        wait_bytes(cmat_in, cm_r)
        c = cmat_in[...]
        dots = jnp.sum(made.astype(F32) * c, axis=1, keepdims=True)
        stat[...] = jnp.sum(jnp.where(diag_low, dots, 0.0), axis=0, keepdims=True)
        send_stat()
        grad = nt(summed, c, HIGHEST)
        a_grad = jnp.zeros((M, M), F32)
        for k in range(ITERS - 1, -1, -1):
            turned = nn(lefts[k], grad, HIGHEST)
            parts = [turned[i * M : (i + 1) * M] for i in range(6)]
            a_grad = a_grad + nn(jnp.concatenate(parts[3:], axis=1), sides[k], HIGHEST)
            grad = nn(jnp.concatenate([grad] + parts[:3], axis=1), steps[k], HIGHEST)
        a_grad = a_grad + grad.T / divisor
        a_score = a * (a_grad - jnp.sum(a * a_grad, axis=1, keepdims=True))
        asc_s[0] = nn(a_score, kl_own.astype(F32), HIGHEST) * SCALE
        asc_s[1] = nn(a_score.T, ql_own.astype(F32), HIGHEST) * SCALE

    shared, trades = {}, []

    def gradients(dx):
        row = lax.rem(x + NX - dx, NX) * NY
        slots = pl.ds(row * NC, NY * NC - (1 if dx == 0 else 0))
        wait_bytes(sb.at[slots], e3t_r.at[dx])
        shared[dx].wait_recv()
        heads = [row + j for j in range(NY)]
        alphas = []
        for h in heads:
            both = sb[NC * h]
            shift = jnp.exp(jnp.where(low, mt_s[h] - both, 0.0))
            alphas.append(jnp.where(low, shift * pltpu.roll(both, M, 1), 0.0))
        dots = [sb[NC * h + 1] for h in heads]
        cols = nt(eye_low, jnp.concatenate(alphas + dots, axis=0), HIGHEST)
        fgs = [nt(ab[0, h], g_v[:, head_cols(h)]) for h in heads]
        bgs = [nt(ab[1, h], v_v[:, head_cols(h)]) for h in heads]
        outs = []
        for j, (h, fg, bg) in enumerate(zip(heads, fgs, bgs)):
            fp = f_s[h]
            fs = (fp * (fg - jnp.sum(fp * fg, axis=0, keepdims=True))).astype(BF)
            bp = w_s[h] * cols[:, j : j + 1]
            bs = (bp * (bg - cols[:, NY + j : NY + j + 1])).astype(BF)
            kp = nn(fs, q_v[:, head_cols(h)]) * SCALE
            qp = nn(bs, k_v[:, head_cols(h)]) * SCALE
            outs.append((fs, bs, bp.astype(BF), qp, kp))
        for h, (fs, bs, bl, qp, kp) in zip(heads, outs):
            fs_s[h] = fs
            bs_s[h] = bs
            bl_s[h] = bl
            gpart[0, h] = qp
            gpart[1, h] = kp
        if dx == 0:

            @pl.when(core == 1)
            def _():
                for which in range(2):
                    gpart[which, chip] = gpart[which, chip] + asc_s[which]

        block = pl.ds(row, NY)
        trade = remote(
            gpart.at[1 - core, block], ginb.at[block], gs_s.at[dx], gs_r.at[dx], partner
        )
        trade.start()
        trades.append((trade, heads))

    for dx in (0, 1, 3, 2):
        shared[dx] = relay_row(ab, e3_s, e3_r, dx)
    for dx in (0, 1, 3, 2):
        gradients(dx)
    for trade, heads in trades:
        trade.wait_recv()
        for h in heads:
            s32[pl.ds(h, M, stride=H), :] = gpart[core, h] + ginb[h]
    for d in range(CHIPS):
        for c in range(NC):
            at = (d * NC + c) * 32
            s16[d, c] = s32[at : at + 32, :].astype(BF)
    r4[core * CHIPS + chip] = s16[chip, core]
    for offset in OFFSETS:
        target = peer(offset)
        remote(
            s16.at[target // NC, lax.rem(target, NC)], r4.at[core * CHIPS + chip],
            e4_s, e4_r, target,
        ).start()

    for h in range(H):
        at = slice(h * DH, (h + 1) * DH)
        att_v[:, at] = tn(f_s[h].astype(BF), ab[0, h]).astype(BF)
        vg_v[:, at] = tn(bl_s[h], ab[1, h]).astype(BF)
    for h in range(H):
        at = slice(h * DH, (h + 1) * DH)
        qg32[:, at] = tn(fs_s[h], kl[h]) * SCALE
        kg32[:, at] = tn(bs_s[h], ql[h]) * SCALE

    wait_bytes(r4.at[0 : GROUP - 1], e4_r)
    for c in range(NC):
        total = r4[c * CHIPS].astype(F32)
        for d in range(1, CHIPS):
            total = total + r4[c * CHIPS + d].astype(F32)
        land[c * 32 : (c + 1) * 32, :] = total * (1.0 / SEG)

    settle(rb, relays, e1_s)
    for swap in swaps:
        swap.wait_send()
    wait_bytes(fin.at[0 : CHIPS - 1], e2_s)

    @pl.when(core == 0)
    def _():
        wait_bytes(mt_f.at[0 : CHIPS - 1], e2t_s)

    @pl.when(core == 1)
    def _():
        for i in range(NX):
            wait_bytes(mt_s.at[pl.ds(0, NY)], mt_ss.at[i])

    settle(ab, list(shared.values()), e3_s)
    for trade, _ in trades:
        trade.wait_send()
    wait_bytes(sb.at[0 : GROUP - 1], e3t_s)
    wait_bytes(r4.at[0 : GROUP - 1], e4_s)


def finish_kernel(att, vg, qg32, kg32, land, att_out, qg_out, kg_out, vg_out, qg, kg, sem):
    copies = []

    def store(src, dst):
        copy = pltpu.make_async_copy(src, dst, sem.at[len(copies)])
        copy.start()
        copies.append(copy)

    store(att, att_out)
    store(vg, vg_out)
    for own, out, made, first in ((qg32, qg_out, qg, 0), (kg32, kg_out, kg, 2 * H)):
        for h in range(H):
            at = slice(h * DH, (h + 1) * DH)
            for seg in range(2):
                here = slice(seg * SEG, (seg + 1) * SEG)
                row = first + seg * H + h
                made[here, at] = (own[here, at] + land[row : row + 1, :]).astype(BF)
        store(made, out)
    for copy in copies:
        copy.wait()


def per_device(queries, keys, values, out_grad):
    shape = (ROWS, WIDTH)
    dma = pltpu.SemaphoreType.DMA
    rows = pltpu.VMEM(shape, BF)
    scratch = (
        [rows] * 4
        + [pltpu.VMEM((64, DH), F32), pltpu.VMEM((64, DH), BF)]
        + [pltpu.VMEM((NC, CHIPS, 64, DH), BF), pltpu.VMEM((2, M * H, DH), F32)]
        + [pltpu.VMEM((H, M, DH), BF)] * 2
        + [pltpu.VMEM((H, M, ROWS), F32)] * 2
        + [pltpu.VMEM((2, H, M, DH), F32)]
        + [pltpu.VMEM((H, M, DH), F32)] * 3
        + [pltpu.VMEM((H, 1, DH), F32)] * 4
        + [pltpu.VMEM((M, DH), F32)]
        + [pltpu.VMEM((ITERS, n * M, M), F32) for n in (6, 4, 3)]
        + [pltpu.VMEM((M, DH), BF), pltpu.VMEM((1, DH), F32)]
        + [pltpu.VMEM((M, DH), F32)] * 2
        + [pltpu.VMEM((NC, CHIPS, M, DH), BF), pltpu.VMEM((GROUP, 1, DH), F32)]
        + [pltpu.VMEM((2, H, M, DH), F32), pltpu.VMEM((H, M, DH), F32)]
        + [pltpu.VMEM((M * H, DH), F32)]
        + [pltpu.VMEM((CHIPS, NC, 32, DH), BF), pltpu.VMEM((GROUP, 32, DH), BF)]
        + [pltpu.VMEM((H, M, ROWS), BF)] * 3
        + [pltpu.VMEM((2, M, DH), F32)]
        + [dma((4,)), dma((NX + 1,)), dma((2 * NX,))]
        + [dma((NX,))] * 4
        + [dma] * 4
        + [dma] * 2
        + [dma((NX + 1,)), dma((2 * NX,)), dma, dma((NX,))]
        + [dma((NX,))] * 2
        + [dma] * 2
    )
    made = pl.pallas_call(
        kernel,
        out_shape=[pltpu.VMEM(shape, BF)] * 2
        + [pltpu.VMEM(shape, F32)] * 2
        + [pltpu.VMEM((64, DH), F32)],
        in_specs=[pl.BlockSpec(memory_space=pl.ANY)] * 4,
        out_specs=[pl.BlockSpec(memory_space=pltpu.VMEM)] * 5,
        scratch_shapes=scratch,
        compiler_params=pltpu.CompilerParams(
            collective_id=0, has_side_effects=True, vmem_limit_bytes=30 << 20
        ),
    )(*[pltpu.with_memory_space_constraint(a, pltpu.HBM) for a in (queries, keys, values, out_grad)])
    return pl.pallas_call(
        finish_kernel,
        out_shape=[jax.ShapeDtypeStruct(shape, BF)] * 4,
        in_specs=[pl.BlockSpec(memory_space=pltpu.VMEM)] * 5,
        out_specs=[pl.BlockSpec(memory_space=pl.ANY)] * 4,
        scratch_shapes=[rows] * 2 + [dma((4,))],
        compiler_params=pltpu.CompilerParams(vmem_limit_bytes=8 << 20),
    )(*made)


def solution(mesh):
    placed = P(("doc", "ctx"), None)
    return jax.shard_map(
        per_device,
        mesh=mesh,
        in_specs=(placed,) * 4,
        out_specs=(placed,) * 4,
        check_vma=False,
    )
```

time: 55.7 us -> 45.9 us (0.82)
  local copies, waits for them, and re-layouts: 5.19 us -> 0 us
  Pallas kernels: 49.6 us -> 45 us
    unnamed x10 -> x0, local copies, waits for them, and re-layouts: 5.19 us -> none
    pallas_call x1 -> x2, Pallas kernels: 49.6 us -> 45 us  [the longest x1 43.6 us: per_device(): pl.pallas_call(kernel, out_shape=[pltpu.VMEM(shape, BF)] * 2 + [pltpu.VME...]
where the time goes in v2:
time: 45.9 us; the launch traced here: 45.8 us
  Pallas kernels  45 us (98%)
  between operations  0.8 us (2%)
    pallas_call x1, Pallas kernels, per_device(): pl.pallas_call(kernel, out_shape=[pltpu.VMEM(shape, BF)] * 2 + [pltpu.VME...  43.6 us
    pallas_call x1, Pallas kernels, per_device(): pl.pallas_call(finish_kernel, out_shape=[jax.ShapeDtypeStruct(shape, BF)]...  1.35 us

profile of v2, /device:TPU:1, one launch (start us, length us, event | category | flops | bytes accessed | tf_op | source)
XLA Modules:
  0.0 45.8 jit_solution(16531430258274807330)
XLA Ops:
  0.6 43.6 %shard_map.75 = (bf16[128,2048]{1,0:T(8,128)(2,1)S(1)}, bf16[128,2048]{1,0:T(8,128)(2,1)S(1)}, f32[128,2048]{1,0:T(8,128)S(1)}, f32[128,2048]{1,0:T(8,128)S(1)}, f32[64,128]{1,0:T(8,128)S(1)}) custom-call(bf16[128,2048]{1,0:T(8,128)(2,1)} %q_hbm.1, bf16[128,2048]{1,0:T(8,128)(2,1)} %k_hbm.1, bf16[128,2048]{1,0:T(8,128)(2,1)} %v_hbm.1, bf16[128,2048]{1,0:T(8,128)(2,1)} %g_hbm.1), custom_call_target="tpu_custom_call" | custom-call | tf_op jit(solution)/shard_map/pallas_call | solution.py:533
  44.3 1.3 %shard_map.76 = (bf16[128,2048]{1,0:T(8,128)(2,1)}, bf16[128,2048]{1,0:T(8,128)(2,1)}, bf16[128,2048]{1,0:T(8,128)(2,1)}, bf16[128,2048]{1,0:T(8,128)(2,1)}) custom-call(bf16[128,2048]{1,0:T(8,128)(2,1)S(1)} %get-tuple-element.9.att, bf16[128,2048]{1,0:T(8,128)(2,1)S(1)} %get-tuple-element.10.vg, f32[128,2048]{1,0:T(8,128)S(1)} %get-tuple-element.11.qg32, ...), custom_call_target="tpu_custom_call" | custom-call | tf_op jit(solution)/shard_map/pallas_call | solution.py:545

commit v3 on v2

v3 whole, which is shorter than its diff:
```python
import jax
import jax.numpy as jnp
from jax import lax
from jax.experimental import pallas as pl
from jax.experimental.pallas import tpu as pltpu
from jax.sharding import PartitionSpec as P

H = 16
DH = 128
M = 64
ITERS = 6
SCALE = DH ** (-0.5)
MESH = pl.DeviceIdType.MESH
HIGHEST = lax.Precision.HIGHEST
BF = jnp.bfloat16
F32 = jnp.float32
NX, NY, NC = 4, 4, 2
CHIPS = NX * NY
GROUP = CHIPS * NC
ROWS = 128
SEG = 64
WIDTH = H * DH

STEPS = [
    (2, 2), (2, 1), (1, 2), (2, 3), (3, 2), (2, 0), (0, 2), (1, 1),
    (3, 3), (1, 3), (3, 1), (1, 0), (0, 1), (3, 0), (0, 3), (0, 0),
]
OTHERS = STEPS[:-1]
OFFSETS = [(dx, dy, dc) for dx, dy in OTHERS for dc in range(NC)] + [(0, 0, 1)]


def nn(a, b, precision=None):
    return lax.dot_general(
        a, b, (((1,), (0,)), ((), ())), precision=precision, preferred_element_type=F32
    )


def nt(a, b, precision=None):
    return lax.dot_general(
        a, b, (((1,), (1,)), ((), ())), precision=precision, preferred_element_type=F32
    )


def tn(a, b, precision=None):
    return lax.dot_general(
        a, b, (((0,), (0,)), ((), ())), precision=precision, preferred_element_type=F32
    )


def iota(shape, dim):
    return lax.broadcasted_iota(jnp.int32, shape, dim)


def wait_bytes(ref, sem):
    pltpu.make_async_copy(ref, ref, sem).wait()


def head_cols(h):
    return pl.ds(pl.multiple_of(h * DH, DH), DH)


def kernel(
    q_hbm, k_hbm, v_hbm, g_hbm,
    att_v, vg_v, qg32, kg32, land,
    q_v, k_v, a_v, b_v,
    msg32, msg16, rb, lf, lm, lm_in,
    w_s, part, fin, mt_s, mt_f, sum_s,
    lefts, steps, sides,
    res, stat, cmat_in, cmat_out, ab, sb,
    s32, s16, r4, bs_s, bl_s, asc_out, asc_in, asc_s, x1_s, x2_s,
    in_sem, pre_s, pre_r, e1_s, e1_r, lm_ss, lm_sr, e2_s, e2_r, e2t_s, e2t_r,
    cm_s, cm_r, e3_s, e3_r, e3t_s, e3t_r, as_s, as_r, e4_s, e4_r, x_s, x_r,
):
    me = lax.axis_index("ctx")
    core = lax.rem(me, NC)
    chip = me // NC
    y = lax.rem(chip, NY)
    x = chip // NY
    partner = chip * NC + (1 - core)

    def chip_at(dx, dy):
        return lax.rem(x + dx, NX) * NY + lax.rem(y + dy, NY)

    def peer(offset):
        dx, dy, dc = offset
        return chip_at(dx, dy) * NC + lax.rem(core + dc, NC)

    def remote(src, dst, send, recv, target):
        return pltpu.make_async_remote_copy(
            src_ref=src, dst_ref=dst, send_sem=send, recv_sem=recv,
            device_id={"ctx": target}, device_id_type=MESH,
        )

    barrier = pltpu.get_barrier_semaphore()
    for offset in OFFSETS:
        pl.semaphore_signal(
            barrier, inc=1, device_id={"ctx": peer(offset)}, device_id_type=MESH
        )
    load_q = pltpu.make_async_copy(q_hbm, q_v, in_sem.at[0])
    load_k = pltpu.make_async_copy(k_hbm, k_v, in_sem.at[1])
    load_q.start()
    load_k.start()
    mine = pl.ds(pl.multiple_of(core * ROWS, ROWS), ROWS)

    @pl.when(core == 0)
    def _():
        pltpu.make_async_copy(k_hbm, a_v.at[0:ROWS], in_sem.at[2]).start()
        pltpu.make_async_copy(v_hbm, b_v.at[0:ROWS], in_sem.at[3]).start()

    @pl.when(core == 1)
    def _():
        pltpu.make_async_copy(q_hbm, a_v.at[ROWS : 2 * ROWS], in_sem.at[2]).start()
        pltpu.make_async_copy(g_hbm, b_v.at[ROWS : 2 * ROWS], in_sem.at[3]).start()

    pick = jnp.where(iota((8, ROWS), 0) == iota((8, ROWS), 1) // SEG, 1.0, 0.0).astype(BF)
    for which, load, ref in ((0, load_q, q_v), (1, load_k, k_v)):
        load.wait()
        sums = nn(pick, ref[...]) * (1.0 / SEG)
        for seg in range(2):
            for h in range(H):
                row = seg * H + h
                msg32[which, row : row + 1, :] = sums[seg : seg + 1, h * DH : (h + 1) * DH]
    msg16[...] = msg32[...].astype(BF)
    rb[me] = msg16[core]
    pl.semaphore_wait(barrier, GROUP - 1)
    for offset in OFFSETS:
        target = peer(offset)
        remote(msg16.at[lax.rem(target, NC)], rb.at[me], e1_s, e1_r, target).start()

    @pl.when(core == 0)
    def _():
        remote(q_hbm, a_v.at[0:ROWS], pre_s.at[0], pre_r.at[0], partner).start()
        remote(g_hbm, b_v.at[0:ROWS], pre_s.at[1], pre_r.at[1], partner).start()

    @pl.when(core == 1)
    def _():
        remote(k_hbm, a_v.at[ROWS : 2 * ROWS], pre_s.at[0], pre_r.at[0], partner).start()
        remote(v_hbm, b_v.at[ROWS : 2 * ROWS], pre_s.at[1], pre_r.at[1], partner).start()

    wait_bytes(a_v.at[mine], in_sem.at[2])
    wait_bytes(b_v.at[mine], in_sem.at[3])
    for slot, ref in ((0, a_v), (1, b_v)):
        wait_bytes(ref.at[0:ROWS], pre_r.at[slot])
    wait_bytes(rb.at[0 : GROUP - 1], e1_r)
    for d in range(GROUP):
        lf[d * 32 : (d + 1) * 32, :] = rb[d].astype(F32)
    for h in range(H):
        lm[h] = lf[pl.ds(h, M, stride=H), :].astype(BF)
    hand = remote(lm.at[chip], lm_in, lm_ss, lm_sr, partner)
    hand.start()

    row_at = iota((M, DH), 0)
    lane_at = iota((M, DH), 1)
    diag_low = lane_at == row_at
    diag_high = lane_at == row_at + M
    low = iota((1, DH), 1) < M
    eye_low = jnp.where(diag_low, 1.0, 0.0)

    def value_group(heads):
        scores = [nt(lm[h], a_v[:, head_cols(h)]) * SCALE for h in heads]
        outs = []
        for h, s in zip(heads, scores):
            m = jnp.max(s, axis=1, keepdims=True)
            w = jnp.exp(s - m)
            t = jnp.sum(w, axis=1, keepdims=True)
            hi = w.astype(BF)
            lo = (w - hi.astype(F32)).astype(BF)
            vals = b_v[:, head_cols(h)]
            sums = nn(hi, vals) + nn(lo, vals)
            row = jnp.sum(
                jnp.where(diag_low, m, 0.0) + jnp.where(diag_high, t, 0.0), axis=0, keepdims=True
            )
            outs.append((w, sums, row))
        for h, (w, sums, row) in zip(heads, outs):
            w_s[h] = w
            part[h] = sums
            mt_s[h] = row

    def gradient_group(heads):
        scores = [nt(lm[h], a_v[:, head_cols(h)]) * SCALE for h in heads]
        outs = []
        for h, s in zip(heads, scores):
            e = jnp.exp(s - jnp.max(s, axis=0, keepdims=True))
            prob = e / jnp.sum(e, axis=0, keepdims=True)
            outs.append((prob, nn(prob.astype(BF), b_v[:, head_cols(h)])))
        for h, (prob, sums) in zip(heads, outs):
            w_s[h] = prob
            part[h] = sums

    for i in range(NX):
        group = STEPS[i * NY : (i + 1) * NY]
        heads = [chip_at(*step) for step in group]

        @pl.when(core == 0)
        def _():
            value_group(heads)
            for step, h in zip(group, heads):
                if step == (0, 0):
                    mt_f[chip] = mt_s[h]
                else:
                    remote(mt_s.at[h], mt_f.at[chip], e2t_s, e2t_r, h * NC).start()

        @pl.when(core == 1)
        def _():
            gradient_group(heads)

        for step, h in zip(group, heads):
            if step == (0, 0):
                fin[chip] = part[h]
            else:
                remote(part.at[h], fin.at[chip], e2_s, e2_r, h * NC + core).start()

    hand.wait_recv()
    own = lm[chip].astype(F32)
    other = lm_in[...].astype(F32)
    ql_own = jnp.where(core == 0, own, other)
    kl_own = jnp.where(core == 0, other, own)
    scores = nt(ql_own.astype(BF), kl_own.astype(BF)) * SCALE
    e = jnp.exp(scores - jnp.max(scores, axis=1, keepdims=True))
    a = e / jnp.sum(e, axis=1, keepdims=True)
    divisor = jnp.max(jnp.sum(a, axis=0, keepdims=True), axis=1, keepdims=True) * jnp.max(
        jnp.sum(a, axis=1, keepdims=True), axis=0, keepdims=True
    )
    a_t = a.T
    z = a_t / divisor
    unit = jnp.where(iota((M, M), 0) == iota((M, M), 1), 1.0, 0.0)
    sweeps = []
    for _ in range(ITERS):
        p = nn(a, z, HIGHEST)
        q1 = 7.0 * unit - p
        q2 = 15.0 * unit - nn(p, q1, HIGHEST)
        q3 = 13.0 * unit - nn(p, q2, HIGHEST)
        sweeps.append((z, p, q1, q2, q3))
        z = 0.25 * nn(z, q3, HIGHEST)
    left = jnp.where(core == 0, z, z.T)

    @pl.when(core == 1)
    def _():
        for k, (before, p, q1, q2, q3) in enumerate(sweeps):
            l0 = before.T
            l1 = nn(p, l0, HIGHEST)
            l2 = nn(p, l1, HIGHEST)
            s0, s1, s2 = [nn(a_t, l, HIGHEST) for l in (l0, l1, l2)]
            lefts[k] = jnp.concatenate([s0, s1, s2, l0, l1, l2], axis=0)
            steps[k] = 0.25 * jnp.concatenate([q3, -q2, q1, -unit], axis=0)
            sides[k] = 0.25 * jnp.concatenate(
                [7.0 * l1 - 15.0 * l0 - l2, 7.0 * l0 - l1, -l0], axis=0
            )

    wait_bytes(fin.at[0 : CHIPS - 1], e2_r)

    @pl.when(core == 0)
    def _():
        wait_bytes(mt_f.at[0 : CHIPS - 1], e2t_r)
        rows = jnp.concatenate([mt_f[s] for s in range(CHIPS)], axis=0)
        top = jnp.max(rows, axis=0, keepdims=True)
        factor = jnp.exp(rows - top)
        total = jnp.sum(factor * pltpu.roll(rows, M, 1), axis=0, keepdims=True)
        inverse = jnp.where(low, 1.0 / jnp.where(low, total, 1.0), 0.0)
        weight = nt(eye_low, factor * inverse, HIGHEST)
        summed = fin[0] * weight[:, 0:1]
        for s in range(1, CHIPS):
            summed = summed + fin[s] * weight[:, s : s + 1]
        sum_s[...] = summed
        stat[...] = jnp.where(low, top, pltpu.roll(inverse, M, 1))

    @pl.when(core == 1)
    def _():
        summed = fin[0]
        for s in range(1, CHIPS):
            summed = summed + fin[s]
        sum_s[...] = summed

    summed = sum_s[...]
    made = nn(left, summed, HIGHEST).astype(BF)
    res[...] = made
    for dx, dy in STEPS:
        remote(res, ab.at[chip], e3_s, e3_r.at[dx], peer((dx, dy, 1))).start()

    @pl.when(core == 0)
    def _():
        cmat_out[...] = summed
        remote(cmat_out, cmat_in, cm_s, cm_r, partner).start()
        sb[chip] = stat[...]
        for dx, dy in OTHERS:
            remote(stat, sb.at[chip], e3t_s, e3t_r.at[dx], peer((dx, dy, 0))).start()
        wait_bytes(cmat_out, cm_s)

    @pl.when(core == 1)
    def _():
        wait_bytes(cmat_in, cm_r)
        c = cmat_in[...]
        dots = jnp.sum(made.astype(F32) * c, axis=1, keepdims=True)
        stat[...] = jnp.sum(jnp.where(diag_low, dots, 0.0), axis=0, keepdims=True)
        for dx, dy in STEPS:
            remote(stat, sb.at[CHIPS + chip], e3t_s, e3t_r.at[dx], peer((dx, dy, 1))).start()
        grad = nt(summed, c, HIGHEST)
        a_grad = jnp.zeros((M, M), F32)
        for k in range(ITERS - 1, -1, -1):
            turned = nn(lefts[k], grad, HIGHEST)
            parts = [turned[i * M : (i + 1) * M] for i in range(6)]
            a_grad = a_grad + nn(jnp.concatenate(parts[3:], axis=1), sides[k], HIGHEST)
            grad = nn(jnp.concatenate([grad] + parts[:3], axis=1), steps[k], HIGHEST)
        a_grad = a_grad + grad.T / divisor
        a_score = a * (a_grad - jnp.sum(a * a_grad, axis=1, keepdims=True))
        asc_out[...] = nn(a_score, kl_own, HIGHEST) * SCALE
        remote(asc_out, asc_in, as_s, as_r, partner).start()
        asc_s[...] = nn(a_score.T, ql_own, HIGHEST) * SCALE

    for dx in (0, 1, 3, 2):
        row = lax.rem(x + NX - dx, NX) * NY
        heads = [row + j for j in range(NY)]
        wait_bytes(ab.at[0:NY], e3_r.at[dx])

        @pl.when(core == 0)
        def _():
            wait_bytes(sb.at[0 : (2 * NY - 1 if dx == 0 else 2 * NY)], e3t_r.at[dx])
            alphas = []
            for h in heads:
                both = sb[h]
                shift = jnp.exp(jnp.where(low, mt_s[h] - both, 0.0))
                alphas.append(jnp.where(low, shift * pltpu.roll(both, M, 1), 0.0))
            dots = [sb[CHIPS + h] for h in heads]
            cols = nt(eye_low, jnp.concatenate(alphas + dots, axis=0), HIGHEST)
            grads = [nt(ab[h], b_v[:, head_cols(h)]) for h in heads]
            outs = []
            for j, (h, bg) in enumerate(zip(heads, grads)):
                prob = w_s[h] * cols[:, j : j + 1]
                score = (prob * (bg - cols[:, NY + j : NY + j + 1])).astype(BF)
                outs.append((prob.astype(BF), score, nn(score, a_v[:, head_cols(h)]) * SCALE))
            for h, (prob, score, sums) in zip(heads, outs):
                bl_s[h] = prob
                bs_s[h] = score
                s32[pl.ds(h, M, stride=H), :] = sums

        @pl.when(core == 1)
        def _():
            grads = [nt(ab[h], b_v[:, head_cols(h)]) for h in heads]
            outs = []
            for h, fg in zip(heads, grads):
                prob = w_s[h]
                score = (prob * (fg - jnp.sum(prob * fg, axis=0, keepdims=True))).astype(BF)
                outs.append((prob.astype(BF), score, nn(score, a_v[:, head_cols(h)]) * SCALE))
            for h, (prob, score, sums) in zip(heads, outs):
                bl_s[h] = prob
                bs_s[h] = score
                s32[pl.ds(h, M, stride=H), :] = sums

    @pl.when(core == 0)
    def _():
        wait_bytes(asc_in, as_r)
        asc_s[...] = asc_in[...]

    at_own = pl.ds(chip, M, stride=H)
    s32[at_own, :] = s32[at_own, :] + asc_s[...]
    for d in range(CHIPS):
        for c in range(NC):
            at = (d * NC + c) * 32
            s16[d, c] = s32[at : at + 32, :].astype(BF)
    r4[core * CHIPS + chip] = s16[chip, core]
    for offset in OFFSETS:
        target = peer(offset)
        remote(
            s16.at[target // NC, lax.rem(target, NC)], r4.at[core * CHIPS + chip],
            e4_s, e4_r, target,
        ).start()

    for first in range(0, H, 4):
        for h in range(first, first + 4):
            at = slice(h * DH, (h + 1) * DH)
            part2 = tn(bs_s[h], lm[h]) * SCALE
            part1 = tn(bl_s[h], ab[h]).astype(BF)
            for c in range(NC):
                x2_s[c, :, at] = part2[c * ROWS : (c + 1) * ROWS]
                x1_s[c, :, at] = part1[c * ROWS : (c + 1) * ROWS]
        cols = pl.ds(first * DH, 4 * DH)

        def move(kept1, kept2, given1, given2, c):
            for slot, (src, kept, given) in enumerate(
                ((x1_s, kept1, given1), (x2_s, kept2, given2))
            ):
                remote(
                    src.at[1 - c, :, cols], given.at[:, cols], x_s.at[slot], x_r.at[slot], partner
                ).start()
                pltpu.make_async_copy(
                    src.at[c, :, cols], kept.at[:, cols], x_s.at[2 + slot]
                ).start()

        @pl.when(core == 0)
        def _():
            move(vg_v, kg32, vg_v, kg32, 0)

        @pl.when(core == 1)
        def _():
            move(att_v, qg32, att_v, qg32, 1)

    wait_bytes(r4.at[0 : GROUP - 1], e4_r)
    for c in range(NC):
        total = r4[c * CHIPS].astype(F32)
        for d in range(1, CHIPS):
            total = total + r4[c * CHIPS + d].astype(F32)
        land[c * 32 : (c + 1) * 32, :] = total * (1.0 / SEG)

    for slot, ref in ((0, x1_s), (1, x2_s)):
        wait_bytes(ref.at[0], x_r.at[slot])
        wait_bytes(ref.at[0], x_s.at[slot])
        wait_bytes(ref.at[0], x_s.at[2 + slot])
    for slot, ref in ((0, a_v), (1, b_v)):
        wait_bytes(ref.at[0:ROWS], pre_s.at[slot])
    wait_bytes(rb.at[0 : GROUP - 1], e1_s)
    hand.wait_send()
    wait_bytes(fin.at[0 : CHIPS - 1], e2_s)
    wait_bytes(ab.at[0:CHIPS], e3_s)

    @pl.when(core == 0)
    def _():
        wait_bytes(mt_f.at[0 : CHIPS - 1], e2t_s)
        wait_bytes(sb.at[0 : CHIPS - 1], e3t_s)

    @pl.when(core == 1)
    def _():
        wait_bytes(sb.at[0:CHIPS], e3t_s)
        wait_bytes(asc_out, as_s)

    wait_bytes(r4.at[0 : GROUP - 1], e4_s)


def finish_kernel(att, vg, qg32, kg32, land, att_out, qg_out, kg_out, vg_out, qg, kg, sem):
    copies = []

    def store(src, dst):
        copy = pltpu.make_async_copy(src, dst, sem.at[len(copies)])
        copy.start()
        copies.append(copy)

    store(att, att_out)
    store(vg, vg_out)
    for own, out, made, first in ((qg32, qg_out, qg, 0), (kg32, kg_out, kg, 2 * H)):
        for h in range(H):
            at = slice(h * DH, (h + 1) * DH)
            for seg in range(2):
                here = slice(seg * SEG, (seg + 1) * SEG)
                row = first + seg * H + h
                made[here, at] = (own[here, at] + land[row : row + 1, :]).astype(BF)
        store(made, out)
    for copy in copies:
        copy.wait()


def per_device(queries, keys, values, out_grad):
    shape = (ROWS, WIDTH)
    dma = pltpu.SemaphoreType.DMA
    rows = pltpu.VMEM(shape, BF)
    square = pltpu.VMEM((M, DH), F32)
    scratch = (
        [rows] * 2
        + [pltpu.VMEM((NC * ROWS, WIDTH), BF)] * 2
        + [pltpu.VMEM((2, 32, DH), F32), pltpu.VMEM((2, 32, DH), BF)]
        + [pltpu.VMEM((GROUP, 32, DH), BF), pltpu.VMEM((M * H, DH), F32)]
        + [pltpu.VMEM((H, M, DH), BF), pltpu.VMEM((M, DH), BF)]
        + [pltpu.VMEM((H, M, NC * ROWS), F32)]
        + [pltpu.VMEM((H, M, DH), F32)] * 2
        + [pltpu.VMEM((H, 1, DH), F32)] * 2
        + [square]
        + [pltpu.VMEM((ITERS, n * M, M), F32) for n in (6, 4, 3)]
        + [pltpu.VMEM((M, DH), BF), pltpu.VMEM((1, DH), F32)]
        + [square] * 2
        + [pltpu.VMEM((CHIPS, M, DH), BF), pltpu.VMEM((GROUP, 1, DH), F32)]
        + [pltpu.VMEM((M * H, DH), F32)]
        + [pltpu.VMEM((CHIPS, NC, 32, DH), BF), pltpu.VMEM((GROUP, 32, DH), BF)]
        + [pltpu.VMEM((H, M, NC * ROWS), BF)] * 2
        + [square] * 3
        + [pltpu.VMEM((NC,) + shape, BF), pltpu.VMEM((NC,) + shape, F32)]
        + [dma((4,)), dma((2,)), dma((2,))]
        + [dma] * 8
        + [dma] * 2
        + [dma, dma((NX,)), dma, dma((NX,))]
        + [dma] * 4
        + [dma((4,)), dma((2,))]
    )
    made = pl.pallas_call(
        kernel,
        out_shape=[pltpu.VMEM(shape, BF)] * 2
        + [pltpu.VMEM(shape, F32)] * 2
        + [pltpu.VMEM((64, DH), F32)],
        in_specs=[pl.BlockSpec(memory_space=pl.ANY)] * 4,
        out_specs=[pl.BlockSpec(memory_space=pltpu.VMEM)] * 5,
        scratch_shapes=scratch,
        compiler_params=pltpu.CompilerParams(
            collective_id=0, has_side_effects=True, vmem_limit_bytes=30 << 20
        ),
    )(*[pltpu.with_memory_space_constraint(a, pltpu.HBM) for a in (queries, keys, values, out_grad)])
    return pl.pallas_call(
        finish_kernel,
        out_shape=[jax.ShapeDtypeStruct(shape, BF)] * 4,
        in_specs=[pl.BlockSpec(memory_space=pltpu.VMEM)] * 5,
        out_specs=[pl.BlockSpec(memory_space=pl.ANY)] * 4,
        scratch_shapes=[rows] * 2 + [dma((4,))],
        compiler_params=pltpu.CompilerParams(vmem_limit_bytes=8 << 20),
    )(*made)


def solution(mesh):
    placed = P(("doc", "ctx"), None)
    return jax.shard_map(
        per_device,
        mesh=mesh,
        in_specs=(placed,) * 4,
        out_specs=(placed,) * 4,
        check_vma=False,
    )
```

time: 45.9 us -> 38.8 us (0.85)
  Pallas kernels: 45 us -> 37.9 us
    pallas_call x1, Pallas kernels: 43.6 us -> 36.5 us  [per_device(): pl.pallas_call(kernel, out_shape=[pltpu.VMEM(shape, BF)] * 2 + [pltpu.VME...]
where the time goes in v3:
time: 38.8 us; the launch traced here: 38.7 us
  Pallas kernels  37.9 us (98%)
  between operations  0.8 us (2%)
    pallas_call x1, Pallas kernels, per_device(): pl.pallas_call(kernel, out_shape=[pltpu.VMEM(shape, BF)] * 2 + [pltpu.VME...  36.5 us
    pallas_call x1, Pallas kernels, per_device(): pl.pallas_call(finish_kernel, out_shape=[jax.ShapeDtypeStruct(shape, BF)]...  1.35 us

profile of v3, /device:TPU:1, one launch (start us, length us, event | category | flops | bytes accessed | tf_op | source)
XLA Modules:
  0.0 38.7 jit_solution(5942876947515972468)
XLA Ops:
  0.6 36.5 %shard_map.75 = (bf16[128,2048]{1,0:T(8,128)(2,1)S(1)}, bf16[128,2048]{1,0:T(8,128)(2,1)S(1)}, f32[128,2048]{1,0:T(8,128)S(1)}, f32[128,2048]{1,0:T(8,128)S(1)}, f32[64,128]{1,0:T(8,128)S(1)}) custom-call(bf16[128,2048]{1,0:T(8,128)(2,1)} %q_hbm.1, bf16[128,2048]{1,0:T(8,128)(2,1)} %k_hbm.1, bf16[128,2048]{1,0:T(8,128)(2,1)} %v_hbm.1, bf16[128,2048]{1,0:T(8,128)(2,1)} %g_hbm.1), custom_call_target="tpu_custom_call" | custom-call | tf_op jit(solution)/shard_map/pallas_call | solution.py:481
  37.2 1.3 %shard_map.76 = (bf16[128,2048]{1,0:T(8,128)(2,1)}, bf16[128,2048]{1,0:T(8,128)(2,1)}, bf16[128,2048]{1,0:T(8,128)(2,1)}, bf16[128,2048]{1,0:T(8,128)(2,1)}) custom-call(bf16[128,2048]{1,0:T(8,128)(2,1)S(1)} %get-tuple-element.9.att, bf16[128,2048]{1,0:T(8,128)(2,1)S(1)} %get-tuple-element.10.vg, f32[128,2048]{1,0:T(8,128)S(1)} %get-tuple-element.11.qg32, ...), custom_call_target="tpu_custom_call" | custom-call | tf_op jit(solution)/shard_map/pallas_call | solution.py:493

commit v4 on v3

--- a/solution.py
+++ b/solution.py
@@ -45,6 +45,16 @@
     return lax.dot_general(
         a, b, (((0,), (0,)), ((), ())), precision=precision, preferred_element_type=F32
     )
+
+
+def halves(a):
+    hi = a.astype(BF)
+    return hi, (a - hi.astype(F32)).astype(BF)
+
+
+def by_halves(blocks, right_hi, right_lo):
+    hi, lo = halves(jnp.concatenate(blocks, axis=1))
+    return nn(hi, right_hi) + (nn(lo, right_hi) + nn(hi, right_lo))
 
 
 def iota(shape, dim):
@@ -241,10 +251,14 @@
             l1 = nn(p, l0, HIGHEST)
             l2 = nn(p, l1, HIGHEST)
             s0, s1, s2 = [nn(a_t, l, HIGHEST) for l in (l0, l1, l2)]
-            lefts[k] = jnp.concatenate([s0, s1, s2, l0, l1, l2], axis=0)
-            steps[k] = 0.25 * jnp.concatenate([q3, -q2, q1, -unit], axis=0)
-            sides[k] = 0.25 * jnp.concatenate(
-                [7.0 * l1 - 15.0 * l0 - l2, 7.0 * l0 - l1, -l0], axis=0
+            hi, lo = halves(jnp.concatenate([s0, s1, s2, l0, l1, l2], axis=0))
+            lefts[k] = jnp.concatenate([hi, hi, lo], axis=1)
+            steps[0, k], steps[1, k] = halves(
+                0.25 * jnp.concatenate([q3, -q2, q1, -unit], axis=0)
+            )
+            sides[0, k], sides[1, k] = halves(
+                0.25
+                * jnp.concatenate([7.0 * l1 - 15.0 * l0 - l2, 7.0 * l0 - l1, -l0], axis=0)
             )
 
     wait_bytes(fin.at[0 : CHIPS - 1], e2_r)
@@ -262,6 +276,8 @@
         for s in range(1, CHIPS):
             summed = summed + fin[s] * weight[:, s : s + 1]
         sum_s[...] = summed
+        cmat_out[...] = summed
+        remote(cmat_out, cmat_in, cm_s, cm_r, partner).start()
         stat[...] = jnp.where(low, top, pltpu.roll(inverse, M, 1))
 
     @pl.when(core == 1)
@@ -279,8 +295,6 @@
 
     @pl.when(core == 0)
     def _():
-        cmat_out[...] = summed
-        remote(cmat_out, cmat_in, cm_s, cm_r, partner).start()
         sb[chip] = stat[...]
         for dx, dy in OTHERS:
             remote(stat, sb.at[chip], e3t_s, e3t_r.at[dx], peer((dx, dy, 0))).start()
@@ -297,10 +311,11 @@
         grad = nt(summed, c, HIGHEST)
         a_grad = jnp.zeros((M, M), F32)
         for k in range(ITERS - 1, -1, -1):
-            turned = nn(lefts[k], grad, HIGHEST)
+            hi, lo = halves(grad)
+            turned = nn(lefts[k], jnp.concatenate([hi, lo, hi], axis=0))
             parts = [turned[i * M : (i + 1) * M] for i in range(6)]
-            a_grad = a_grad + nn(jnp.concatenate(parts[3:], axis=1), sides[k], HIGHEST)
-            grad = nn(jnp.concatenate([grad] + parts[:3], axis=1), steps[k], HIGHEST)
+            grad = by_halves([grad] + parts[:3], steps[0, k], steps[1, k])
+            a_grad = a_grad + by_halves(parts[3:], sides[0, k], sides[1, k])
         a_grad = a_grad + grad.T / divisor
         a_score = a * (a_grad - jnp.sum(a * a_grad, axis=1, keepdims=True))
         asc_out[...] = nn(a_score, kl_own, HIGHEST) * SCALE
@@ -462,7 +477,8 @@
         + [pltpu.VMEM((H, M, DH), F32)] * 2
         + [pltpu.VMEM((H, 1, DH), F32)] * 2
         + [square]
-        + [pltpu.VMEM((ITERS, n * M, M), F32) for n in (6, 4, 3)]
+        + [pltpu.VMEM((ITERS, 6 * M, 3 * M), BF)]
+        + [pltpu.VMEM((2, ITERS, n * M, M), BF) for n in (4, 3)]
         + [pltpu.VMEM((M, DH), BF), pltpu.VMEM((1, DH), F32)]
         + [square] * 2
         + [pltpu.VMEM((CHIPS, M, DH), BF), pltpu.VMEM((GROUP, 1, DH), F32)]

time: 38.8 us -> 37.4 us (0.964)
  Pallas kernels: 37.9 us -> 36.6 us
    pallas_call x1, Pallas kernels: 36.5 us -> 35.3 us  [per_device(): pl.pallas_call(kernel, out_shape=[pltpu.VMEM(shape, BF)] * 2 + [pltpu.VME...]
where the time goes in v4:
time: 37.4 us; the launch traced here: 37.3 us
  Pallas kernels  36.6 us (98%)
  between operations  0.64 us (2%)
    pallas_call x1, Pallas kernels, per_device(): pl.pallas_call(kernel, out_shape=[pltpu.VMEM(shape, BF)] * 2 + [pltpu.VME...  35.3 us
    pallas_call x1, Pallas kernels, per_device(): pl.pallas_call(finish_kernel, out_shape=[jax.ShapeDtypeStruct(shape, BF)]...  1.35 us

profile of v4, /device:TPU:1, one launch (start us, length us, event | category | flops | bytes accessed | tf_op | source)
XLA Modules:
  0.0 37.3 jit_solution(11541339884024075761)
XLA Ops:
  0.6 35.3 %shard_map.75 = (bf16[128,2048]{1,0:T(8,128)(2,1)S(1)}, bf16[128,2048]{1,0:T(8,128)(2,1)S(1)}, f32[128,2048]{1,0:T(8,128)S(1)}, f32[128,2048]{1,0:T(8,128)S(1)}, f32[64,128]{1,0:T(8,128)S(1)}) custom-call(bf16[128,2048]{1,0:T(8,128)(2,1)} %q_hbm.1, bf16[128,2048]{1,0:T(8,128)(2,1)} %k_hbm.1, bf16[128,2048]{1,0:T(8,128)(2,1)} %v_hbm.1, bf16[128,2048]{1,0:T(8,128)(2,1)} %g_hbm.1), custom_call_target="tpu_custom_call" | custom-call | tf_op jit(solution)/shard_map/pallas_call | solution.py:497
  35.9 1.3 %shard_map.76 = (bf16[128,2048]{1,0:T(8,128)(2,1)}, bf16[128,2048]{1,0:T(8,128)(2,1)}, bf16[128,2048]{1,0:T(8,128)(2,1)}, bf16[128,2048]{1,0:T(8,128)(2,1)}) custom-call(bf16[128,2048]{1,0:T(8,128)(2,1)S(1)} %get-tuple-element.9.att, bf16[128,2048]{1,0:T(8,128)(2,1)S(1)} %get-tuple-element.10.vg, f32[128,2048]{1,0:T(8,128)S(1)} %get-tuple-element.11.qg32, ...), custom_call_target="tpu_custom_call" | custom-call | tf_op jit(solution)/shard_map/pallas_call | solution.py:509

commit v5 on v4

--- a/solution.py
+++ b/solution.py
@@ -368,13 +368,11 @@
 
     at_own = pl.ds(chip, M, stride=H)
     s32[at_own, :] = s32[at_own, :] + asc_s[...]
-    for d in range(CHIPS):
-        for c in range(NC):
-            at = (d * NC + c) * 32
-            s16[d, c] = s32[at : at + 32, :].astype(BF)
-    r4[core * CHIPS + chip] = s16[chip, core]
+    r4[core * CHIPS + chip] = s32[pl.ds(pl.multiple_of(me * 32, 32), 32), :].astype(BF)
     for offset in OFFSETS:
         target = peer(offset)
+        block = s32[pl.ds(pl.multiple_of(target * 32, 32), 32), :]
+        s16[target // NC, lax.rem(target, NC)] = block.astype(BF)
         remote(
             s16.at[target // NC, lax.rem(target, NC)], r4.at[core * CHIPS + chip],
             e4_s, e4_r, target,
@@ -457,7 +455,9 @@
                 here = slice(seg * SEG, (seg + 1) * SEG)
                 row = first + seg * H + h
                 made[here, at] = (own[here, at] + land[row : row + 1, :]).astype(BF)
-        store(made, out)
+            if h % 8 == 7:
+                done = pl.ds((h - 7) * DH, 8 * DH)
+                store(made.at[:, done], out.at[:, done])
     for copy in copies:
         copy.wait()
 
@@ -511,7 +511,7 @@
         out_shape=[jax.ShapeDtypeStruct(shape, BF)] * 4,
         in_specs=[pl.BlockSpec(memory_space=pltpu.VMEM)] * 5,
         out_specs=[pl.BlockSpec(memory_space=pl.ANY)] * 4,
-        scratch_shapes=[rows] * 2 + [dma((4,))],
+        scratch_shapes=[rows] * 2 + [dma((6,))],
         compiler_params=pltpu.CompilerParams(vmem_limit_bytes=8 << 20),
     )(*made)
 

time: 37.4 us -> 37.4 us (level)
  no operation moved by 1% of the time
where the time goes in v5:
time: 37.4 us; the launch traced here: 37.3 us
  Pallas kernels  36.6 us (98%)
  between operations  0.64 us (2%)
    pallas_call x1, Pallas kernels, per_device(): pl.pallas_call(kernel, out_shape=[pltpu.VMEM(shape, BF)] * 2 + [pltpu.VME...  35.3 us
    pallas_call x1, Pallas kernels, per_device(): pl.pallas_call(finish_kernel, out_shape=[jax.ShapeDtypeStruct(shape, BF)]...  1.36 us

profile of v5, /device:TPU:1, one launch (start us, length us, event | category | flops | bytes accessed | tf_op | source)
XLA Modules:
  0.0 37.3 jit_solution(17785715645675139114)
XLA Ops:
  0.6 35.3 %shard_map.75 = (bf16[128,2048]{1,0:T(8,128)(2,1)S(1)}, bf16[128,2048]{1,0:T(8,128)(2,1)S(1)}, f32[128,2048]{1,0:T(8,128)S(1)}, f32[128,2048]{1,0:T(8,128)S(1)}, f32[64,128]{1,0:T(8,128)S(1)}) custom-call(bf16[128,2048]{1,0:T(8,128)(2,1)} %q_hbm.1, bf16[128,2048]{1,0:T(8,128)(2,1)} %k_hbm.1, bf16[128,2048]{1,0:T(8,128)(2,1)} %v_hbm.1, bf16[128,2048]{1,0:T(8,128)(2,1)} %g_hbm.1), custom_call_target="tpu_custom_call" | custom-call | tf_op jit(solution)/shard_map/pallas_call | solution.py:497
  35.9 1.4 %shard_map.76 = (bf16[128,2048]{1,0:T(8,128)(2,1)}, bf16[128,2048]{1,0:T(8,128)(2,1)}, bf16[128,2048]{1,0:T(8,128)(2,1)}, bf16[128,2048]{1,0:T(8,128)(2,1)}) custom-call(bf16[128,2048]{1,0:T(8,128)(2,1)S(1)} %get-tuple-element.9.att, bf16[128,2048]{1,0:T(8,128)(2,1)S(1)} %get-tuple-element.10.vg, f32[128,2048]{1,0:T(8,128)S(1)} %get-tuple-element.11.qg32, ...), custom_call_target="tpu_custom_call" | custom-call | tf_op jit(solution)/shard_map/pallas_call | solution.py:509
